TPU v7x, 256 devices: a whole 4x4x8 slice. The times are simulated.
256 devices in a mesh: rep: 2 (over z_hi), shard: 128 (over y, z_lo, x, core).
Axes of the slice: x: 4, y: 4, z: 8 (z_hi: 2, z_lo: 4; z = z_hi * 4 + z_lo), core: 2. Of those that a mesh axis runs over, the one named last changes fastest.
Arguments:
- old_master: float32 [655360, 128], P('shard'), may hold values from -100 to 100
- old_first: float32 [655360, 128], P('shard'), may hold values from -6 to 6
- old_second: float32 [655360, 128], P('shard'), may hold values from 0 to 1, as said below
- grad_parts: float32 [2, 393216, 128], P('rep', 'shard'), may hold values from -6 to 6
- old_offsets: int32 [65], replicated, may hold values from 0 to 262144, as said below
- new_offsets: int32 [129], replicated, may hold values from 0 to 262144, as said below
Outputs:
- new_master: float32 [128, 2, 1536, 128], P('shard', 'rep')
- new_first: float32 [128, 2, 1536, 128], P('shard', 'rep')
- new_second: float32 [128, 2, 1536, 128], P('shard', 'rep')
- new_weights: bfloat16 [393216, 128], P('shard')
Inputs may be any that keep to these rules, and one draw needn't show every extreme that they name: `old_offsets`: Rising; starts at 0 and ends at 262144; entry o lies within 512 of 2 * 2048 * o, and at least one old owner holds 5120 rows, the most that any can hold. Old owner o's rows are on shard index 2 * o; odd shard indices hold no old rows. `new_offsets`: Rising; starts at 0 and ends at 262144; entry i lies within 512 of 2048 * i, and at least one new owner holds 3072 rows, the most that any can hold. `old_second`: every entry is positive.
All inputs are finite; a program needn't handle non-finite values.
Results may differ from a plain program's by a relative error of at most 0.001.
Values may be sent and summed in bfloat16 or wider, within the bound.
A program may use at most 128 MiB of HBM per device.

v0:
```python
import jax
import jax.numpy as jnp
from jax import lax
from jax.sharding import PartitionSpec as P

STEP = 10


def from_behind(x, axis, by):
    size = lax.axis_size(axis)
    pairs = [(i, i + by) for i in range(size) if 0 <= i + by < size]
    return lax.ppermute(x, axis, pairs)


def adam_update(master, first, second, grads, valid):
    first_n = 0.9 * first + 0.1 * grads
    second_n = 0.95 * second + 0.05 * grads * grads
    first_hat = first_n / (1.0 - 0.9**STEP)
    second_hat = second_n / (1.0 - 0.95**STEP)
    master_n = master - 0.02 * (first_hat / (jnp.sqrt(second_hat) + 1e-08) + 0.1 * master)
    keep = valid[:, None]
    return (
        jnp.where(keep, master_n, 0.0),
        jnp.where(keep, first_n, 0.0),
        jnp.where(keep, second_n, 0.0),
    )


def send_rows(sent, offset):
    return from_behind(sent, "shard", offset)


def local(old_master, old_first, old_second, grad_parts, old_offsets, new_offsets):
    shard = lax.axis_index("shard")
    replica = lax.axis_index("rep")
    count = lax.axis_size("shard")
    old_cap = old_master.shape[0]
    lanes = old_master.shape[1]
    new_cap = grad_parts.shape[1]
    half = new_cap // lax.axis_size("rep")
    owner = shard // 2
    old_start = old_offsets[owner]
    old_stop = jnp.where(shard % 2 == 0, old_offsets[owner + 1], old_start)
    base = 0
    padded = tuple(
        (
            jnp.concatenate(
                [
                    jnp.zeros((new_cap, lanes), jnp.float32),
                    state,
                    jnp.zeros((new_cap, lanes), jnp.float32),
                ],
                0,
            )
            for state in (old_master, old_first, old_second)
        )
    )

    def window_start(target, offset, extent):
        if offset == -1:
            lead = new_offsets[target + 1] - new_offsets[target] - extent
        else:
            lead = jnp.zeros((), jnp.int32)
        return jnp.clip(lead, base, base + new_cap - extent)

    def rows_for(target, offset, extent):
        target = jnp.clip(target, 0, count - 1)
        first_new = new_offsets[target]
        begin = window_start(target, offset, extent)
        flat_rows = first_new + begin + jnp.arange(extent, dtype=jnp.int32)
        keep = (
            (flat_rows < new_offsets[target + 1])
            & (flat_rows >= old_start)
            & (flat_rows < old_stop)
        )
        start = jnp.clip(first_new + begin - old_start + new_cap, 0, old_cap + 2 * new_cap - extent)
        return tuple(
            (
                jnp.where(keep[:, None], lax.dynamic_slice_in_dim(block, start, extent, 0), 0.0)
                for block in padded
            )
        )

    moved = rows_for(shard, 0, new_cap)
    for offset in (1, 2, -1):
        extent = new_cap if offset == 1 else new_cap
        arrived = send_rows(rows_for(shard + offset, offset, extent), offset)
        moved = tuple((left + right for left, right in zip(moved, arrived)))
    owned = tuple((lax.dynamic_slice_in_dim(block, replica * half, half, 0) for block in moved))
    grads = lax.psum_scatter(grad_parts, "rep", scatter_dimension=1, tiled=True)[0]
    flat_mine = new_offsets[shard] + replica * half + jnp.arange(half, dtype=jnp.int32)
    valid = flat_mine < new_offsets[shard + 1]
    master_n, first_n, second_n = adam_update(owned[0], owned[1], owned[2], grads, valid)
    weights = lax.all_gather(master_n.astype(jnp.bfloat16), "rep", axis=0, tiled=True)
    return (master_n[None, None], first_n[None, None], second_n[None, None], weights)


def solution(mesh):
    in_specs = (
        P("shard", None),
        P("shard", None),
        P("shard", None),
        P("rep", "shard", None),
        P(),
        P(),
    )
    out_specs = (
        P("shard", "rep", None, None),
        P("shard", "rep", None, None),
        P("shard", "rep", None, None),
        P("shard", None),
    )
    return jax.shard_map(local, mesh=mesh, in_specs=in_specs, out_specs=out_specs, check_vma=False)
```

profile of v0, /device:TPU:8, one launch (start us, length us, event | category | flops | bytes accessed | tf_op | source)
XLA Modules:
  0.0 271.9 jit_solution(8210083352098379884)
XLA Ops:
  7.2 1.8 fusion.27
  10.8 1.4 fusion.28
  18.2 3.3 %fusion.19 = (pred[3072]{0:T(1024)(128)(4,1)S(1)}, pred[3072]{0:T(1024)(128)(4,1)S(1)}) fusion(s32[]{:T(128)} %bitcast.7, s32[]{:T(128)} %bitcast.6, s32[]{:T(128)S(6)} %select_n.115, s32[]{:T(128)} %bitcast.4, s32[]{:T(128)} %bitcast.9, s32[]{:T(128)} %bitcast.8), kind=kLoop, calls=%fused_computation.55 | loop fusion | flops 36864 | bytes 6168 | tf_op jit(solution)/shard_map/and | solution.py:72
  21.6 1.3 broadcast.82
  22.9 7.8 %pad_maximum_fusion = (f32[11264,128]{1,0:T(8,128)S(1)}, f32[11264,128]{1,0:T(8,128)S(1)}, f32[11264,128]{1,0:T(8,128)}) fusion(f32[3072,128]{1,0:T(8,128)} %broadcast.82, f32[5120,128]{1,0:T(8,128)} %param.8, f32[5120,128]{1,0:T(8,128)} %param.7, f32[5120,128]{1,0:T(8,128)} %param.6), kind=kLoop, calls=%fused_computation | loop fusion | flops 8650752 | bytes 26738688 | tf_op jit(solution)/shard_map/concatenate | solution.py:47
  30.7 9.6 %dynamic-slice_select_fusion.8 = (f32[3072,128]{1,0:T(8,128)}, f32[3072,128]{1,0:T(8,128)}, f32[3072,128]{1,0:T(8,128)}, f32[3072,128]{1,0:T(8,128)}, f32[3072,1...) fusion(f32[11264,128]{1,0:T(8,128)} %get-tuple-element.19, ...), kind=kLoop, calls=%fused_computation.14 | loop fusion | flops 3538944 | bytes 28320780 | tf_op jit(solution)/shard_map/jit(_where)/select_n | solution.py:79
  40.3 2.0 collective-permute-start
  42.4 8.4 %collective-permute-start.2 = (f32[3072,128]{1,0:T(8,128)}, f32[3072,128]{1,0:T(8,128)}, u32[]{:S(2)}, u32[]{:S(2)}) collective-permute-start(f32[3072,128]{1,0:T(8,128)} %get-tuple-element.15), channel_id=1, source_target_pairs={{1,0},{2,1},{3,2},{4,3},{5,4},{6,5},{7,6},{8,7},{9,8},{10,9},{11,1... | collective-permute-start | bytes 4718600 | tf_op jit(solution)/shard_map/ppermute | solution.py:12
  50.9 1.9 collective-permute-start.1
  52.8 1.9 collective-permute-start.7
  54.7 4.3 %collective-permute-start.8 = (f32[3072,128]{1,0:T(8,128)}, f32[3072,128]{1,0:T(8,128)}, u32[]{:S(2)}, u32[]{:S(2)}) collective-permute-start(f32[3072,128]{1,0:T(8,128)} %get-tuple-element.21), channel_id=1, source_target_pairs={{1,0},{2,1},{3,2},{4,3},{5,4},{6,5},{7,6},{8,7},{9,8},{10,9},{11,1... | collective-permute-start | bytes 4718600 | tf_op jit(solution)/shard_map/ppermute | solution.py:12
  59.1 14.0 %collective-permute-done = f32[3072,128]{1,0:T(8,128)S(1)} collective-permute-done((f32[3072,128]{1,0:T(8,128)}, f32[3072,128]{1,0:T(8,128)S(1)}, u32[]{:S(2)}, u32[]{:S(2)}) %collective-permute-start) | collective-permute-done | bytes 1572896 | tf_op jit(solution)/shard_map/ppermute | solution.py:12
  73.0 1.9 collective-permute-start.6
  75.0 2.6 collective-permute-start.4
  77.6 34.9 %collective-permute-done.1 = f32[3072,128]{1,0:T(8,128)} collective-permute-done((f32[3072,128]{1,0:T(8,128)}, f32[3072,128]{1,0:T(8,128)}, u32[]{:S(2)}, u32[]{:S(2)}) %collective-permute-start.1) | collective-permute-done | bytes 1572896 | tf_op jit(solution)/shard_map/ppermute | solution.py:12
  112.5 12.9 %collective-permute-start.5 = (f32[3072,128]{1,0:T(8,128)}, f32[3072,128]{1,0:T(8,128)}, u32[]{:S(2)}, u32[]{:S(2)}) collective-permute-start(f32[3072,128]{1,0:T(8,128)} %get-tuple-element.24), channel_id=1, source_target_pairs={{1,0},{2,1},{3,2},{4,3},{5,4},{6,5},{7,6},{8,7},{9,8},{10,9},{11,1... | collective-permute-start | bytes 4718600 | tf_op jit(solution)/shard_map/ppermute | solution.py:12
  125.4 21.1 %collective-permute-done.7 = f32[3072,128]{1,0:T(8,128)} collective-permute-done((f32[3072,128]{1,0:T(8,128)}, f32[3072,128]{1,0:T(8,128)}, u32[]{:S(2)}, u32[]{:S(2)}) %collective-permute-start.7) | collective-permute-done | bytes 1572896 | tf_op jit(solution)/shard_map/ppermute | solution.py:12
  146.5 13.7 %collective-permute-start.3 = (f32[3072,128]{1,0:T(8,128)S(1)}, f32[3072,128]{1,0:T(8,128)}, u32[]{:S(2)}, u32[]{:S(2)}) collective-permute-start(f32[3072,128]{1,0:T(8,128)S(1)} %copy-done.2), channel_id=1, source_target_pairs={{0,1},{1,2},{2,3},{3,4},{4,5},{5,6},{6,7},{7,8},{8,9},{9,10},{10,1... | collective-permute-start | bytes 4718600 | tf_op jit(solution)/shard_map/ppermute | solution.py:12
  162.2 2.0 fusion.17
  164.9 21.4 %collective-permute-done.6 = f32[3072,128]{1,0:T(8,128)} collective-permute-done((f32[3072,128]{1,0:T(8,128)}, f32[3072,128]{1,0:T(8,128)}, u32[]{:S(2)}, u32[]{:S(2)}) %collective-permute-start.6) | collective-permute-done | bytes 1572896 | tf_op jit(solution)/shard_map/ppermute | solution.py:12
  186.4 38.1 %collective-permute-done.3 = f32[3072,128]{1,0:T(8,128)} collective-permute-done((f32[3072,128]{1,0:T(8,128)S(1)}, f32[3072,128]{1,0:T(8,128)}, u32[]{:S(2)}, u32[]{:S(2)}) %collective-permute-start.3) | collective-permute-done | bytes 1572896 | tf_op jit(solution)/shard_map/ppermute | solution.py:12
  224.5 5.3 %fusion.24 = (bf16[1536,128]{1,0:T(8,128)(2,1)S(1)}, f32[1536,128]{1,0:T(8,128)}, f32[1536,128]{1,0:T(8,128)S(1)}, f32[1536,128]{1,0:T(8,128)S(1)}) fusion(f32[3072,128]{1,0:T(8,128)} %collective-permute-done.2, s32[]{:T(128)S(6)} %select_n.123, f32[3072,128]{1,0:T(8,128)} %collective-permute-done.1, f32[3072,128]{1,0:T(8,128)S(1)} %collective-permute-done, ...), kind=kLoop, calls=%fused_computation.61 | loop fusion | flops 5701632 | bytes 12979208 | tf_op jit(solution)/shard_map/convert_element_type | solution.py:94
  229.7 33.0 %all_gather.3 = bf16[3072,128]{1,0:T(8,128)(2,1)S(1)} all-gather(bf16[1536,128]{1,0:T(8,128)(2,1)S(1)} %get-tuple-element.4), channel_id=1, replica_groups=mesh['rep'=2,'shard'=128] {'rep'}, dimensions={0}, use_global_device_ids=true | all-gather | bytes 1179648 | tf_op jit(solution)/shard_map/all_gather | solution.py:94
  262.8 1.4 select_bitcast_fusion
  (17 shorter events, 3.0 us)
Async XLA Ops:
  7.2 217.3 %reduce-scatter.2.cloned.1.call-start = ((), (), s32[]{:S(2)}) async-start(), calls=%async_computation.1 | async-start | bytes 2359296 | tf_op jit(solution)/shard_map/reduce_scatter | solution.py:90
  30.7 9.6 %copy-start = (f32[11264,128]{1,0:T(8,128)}, f32[11264,128]{1,0:T(8,128)S(1)}, u32[]{:S(2)}) copy-start(f32[11264,128]{1,0:T(8,128)S(1)} %get-tuple-element.17) | copy-start | bytes 17301508
  30.7 9.7 %copy-start.1 = (f32[11264,128]{1,0:T(8,128)}, f32[11264,128]{1,0:T(8,128)S(1)}, u32[]{:S(2)}) copy-start(f32[11264,128]{1,0:T(8,128)S(1)} %get-tuple-element.18) | copy-start | bytes 17301508
  40.3 106.1 %copy-start.2 = (f32[3072,128]{1,0:T(8,128)S(1)}, f32[3072,128]{1,0:T(8,128)}, u32[]{:S(2)}) copy-start(f32[3072,128]{1,0:T(8,128)} %get-tuple-element.25) | copy-start | bytes 4718596
  40.3 32.7 %collective-permute-start = (f32[3072,128]{1,0:T(8,128)}, f32[3072,128]{1,0:T(8,128)S(1)}, u32[]{:S(2)}, u32[]{:S(2)}) collective-permute-start(f32[3072,128]{1,0:T(8,128)} %get-tuple-element.14), channel_id=1, source_target_pairs={{0,1},{1,2},{2,3},{3,4},{4,5},{5,6},{6,7},{7,8},{8,9},{9,10},{10,1... | collective-permute-start | bytes 4718600 | tf_op jit(solution)/shard_map/ppermute | solution.py:12
  42.4 32.6 %collective-permute-start.2 = (f32[3072,128]{1,0:T(8,128)}, f32[3072,128]{1,0:T(8,128)}, u32[]{:S(2)}, u32[]{:S(2)}) collective-permute-start(f32[3072,128]{1,0:T(8,128)} %get-tuple-element.15), channel_id=1, source_target_pairs={{1,0},{2,1},{3,2},{4,3},{5,4},{6,5},{7,6},{8,7},{9,8},{10,9},{11,1... | collective-permute-start | bytes 4718600 | tf_op jit(solution)/shard_map/ppermute | solution.py:12
  50.9 61.6 %collective-permute-start.1 = (f32[3072,128]{1,0:T(8,128)}, f32[3072,128]{1,0:T(8,128)}, u32[]{:S(2)}, u32[]{:S(2)}) collective-permute-start(f32[3072,128]{1,0:T(8,128)} %get-tuple-element.16), channel_id=1, source_target_pairs={{0,2},{1,3},{2,4},{3,5},{4,6},{5,7},{6,8},{7,9},{8,10},{9,11},{10,... | collective-permute-start | bytes 4718600 | tf_op jit(solution)/shard_map/ppermute | solution.py:12
  52.8 93.7 %collective-permute-start.7 = (f32[3072,128]{1,0:T(8,128)}, f32[3072,128]{1,0:T(8,128)}, u32[]{:S(2)}, u32[]{:S(2)}) collective-permute-start(f32[3072,128]{1,0:T(8,128)} %get-tuple-element.20), channel_id=1, source_target_pairs={{0,2},{1,3},{2,4},{3,5},{4,6},{5,7},{6,8},{7,9},{8,10},{9,11},{10,... | collective-permute-start | bytes 4718600 | tf_op jit(solution)/shard_map/ppermute | solution.py:12
  54.7 110.2 %collective-permute-start.8 = (f32[3072,128]{1,0:T(8,128)}, f32[3072,128]{1,0:T(8,128)}, u32[]{:S(2)}, u32[]{:S(2)}) collective-permute-start(f32[3072,128]{1,0:T(8,128)} %get-tuple-element.21), channel_id=1, source_target_pairs={{1,0},{2,1},{3,2},{4,3},{5,4},{6,5},{7,6},{8,7},{9,8},{10,9},{11,1... | collective-permute-start | bytes 4718600 | tf_op jit(solution)/shard_map/ppermute | solution.py:12
  73.0 113.3 %collective-permute-start.6 = (f32[3072,128]{1,0:T(8,128)}, f32[3072,128]{1,0:T(8,128)}, u32[]{:S(2)}, u32[]{:S(2)}) collective-permute-start(f32[3072,128]{1,0:T(8,128)} %get-tuple-element.22), channel_id=1, source_target_pairs={{0,1},{1,2},{2,3},{3,4},{4,5},{5,6},{6,7},{7,8},{8,9},{9,10},{10,1... | collective-permute-start | bytes 4718600 | tf_op jit(solution)/shard_map/ppermute | solution.py:12
  75.0 111.4 %collective-permute-start.4 = (f32[3072,128]{1,0:T(8,128)}, f32[3072,128]{1,0:T(8,128)}, u32[]{:S(2)}, u32[]{:S(2)}) collective-permute-start(f32[3072,128]{1,0:T(8,128)} %get-tuple-element.23), channel_id=1, source_target_pairs={{0,2},{1,3},{2,4},{3,5},{4,6},{5,7},{6,8},{7,9},{8,10},{9,11},{10,... | collective-permute-start | bytes 4718600 | tf_op jit(solution)/shard_map/ppermute | solution.py:12
  112.5 73.9 %collective-permute-start.5 = (f32[3072,128]{1,0:T(8,128)}, f32[3072,128]{1,0:T(8,128)}, u32[]{:S(2)}, u32[]{:S(2)}) collective-permute-start(f32[3072,128]{1,0:T(8,128)} %get-tuple-element.24), channel_id=1, source_target_pairs={{1,0},{2,1},{3,2},{4,3},{5,4},{6,5},{7,6},{8,7},{9,8},{10,9},{11,1... | collective-permute-start | bytes 4718600 | tf_op jit(solution)/shard_map/ppermute | solution.py:12
  146.5 78.0 %collective-permute-start.3 = (f32[3072,128]{1,0:T(8,128)S(1)}, f32[3072,128]{1,0:T(8,128)}, u32[]{:S(2)}, u32[]{:S(2)}) collective-permute-start(f32[3072,128]{1,0:T(8,128)S(1)} %copy-done.2), channel_id=1, source_target_pairs={{0,1},{1,2},{2,3},{3,4},{4,5},{5,6},{6,7},{7,8},{8,9},{9,10},{10,1... | collective-permute-start | bytes 4718600 | tf_op jit(solution)/shard_map/ppermute | solution.py:12
Sparse Core Ops, SparseCore 0:
  54.9 49.4 reduce-scatter.1
where the time goes:
time: 274 us; the launch traced here: 272 us
  waiting for transfers between devices  129 us (47%)
  starting transfers between devices  49.9 us (18%)
  blocking collectives  33 us (12%)
  other arithmetic  31.3 us (11%)
  between operations  22.7 us (8%)
  local copies, waits for them, and re-layouts  5.51 us (2%)
    ppermute x9, waiting for transfers between devices, from_behind(): return lax.ppermute(x, axis, pairs)  129 us
    ppermute x9, starting transfers between devices, from_behind(): return lax.ppermute(x, axis, pairs)  49.9 us
    all_gather x1, blocking collectives, local(): lax.all_gather(master_n.astype(jnp.bfloat16), 'rep', axis=0, tiled=True)  33 us
    select_n x1, other arithmetic, rows_for(): jnp.where(keep[:, None], lax.dynamic_slice_in_dim(block, start, extent, 0...  9.56 us
    concatenate x1, other arithmetic, local(): jnp.concatenate([jnp.zeros((new_cap, lanes), jnp.float32), state, jnp.zer...  7.82 us
    and x3, other arithmetic, rows_for(): (flat_rows < new_offsets[target + 1]) & (flat_rows >= old_start)  6.6 us
  transfers between devices with their start and end apart: 10, of which 5 were waited for; matrix products, arithmetic and copies ran while one was open for 1% of the time, Pallas kernels for 0%

commit v1 on v0

v1 whole, which is shorter than its diff:
```python
import functools

import jax
import jax.numpy as jnp
from jax import lax
from jax.experimental import pallas as pl
from jax.experimental.pallas import tpu as pltpu
from jax.sharding import PartitionSpec as P

STEP = 10
MESH = pl.DeviceIdType.MESH
JITTER = 512
EDGE = 2 * JITTER
WINDOW = 3584
CHUNKS = 8
SUB = 64


def within(start):
    return jnp.clip(start, 0, 2 * EDGE)


def kernel(
    old_off,
    new_off,
    old_m,
    old_f,
    old_s,
    grads,
    out_m,
    out_f,
    out_s,
    out_w,
    main,
    alt,
    stage,
    edge,
    mine,
    theirs,
    res,
    wts,
    in_sem,
    mine_sem,
    stage_sem,
    die_sem,
    head_sem,
    tail_sem,
    grad_send,
    grad_recv,
    wts_send,
    wts_recv,
    res_sem,
    own_sem,
):
    olds = (old_m, old_f, old_s)
    outs = (out_m, out_f, out_s)
    old_cap = old_m.shape[0]
    half = mine.shape[0]
    size = half // CHUNKS
    r = lax.axis_index("rep")
    s = lax.axis_index("shard")
    owners = lax.axis_size("shard") // 2
    o = s // 2
    core = s % 2
    even = core == 0
    odd = core == 1
    other = (1 - r, s)

    up_rep = jnp.where(o % 16 == 15, 1 - r, r)
    down_rep = jnp.where(o % 16 == 0, 1 - r, r)
    sends_head = even & (up_rep == 0) & (o < owners - 1)
    gets_head = even & (r == 0) & (o > 0)
    sends_tail = even & (o > 0)
    sends_short = sends_tail & (down_rep == 0)
    sends_long = sends_tail & (down_rep == 1)
    gets_tail = odd & (o < owners - 1)
    gets_short = gets_tail & (r == 0)
    gets_long = gets_tail & (r == 1)
    head_to = (up_rep, lax.rem(s + 2, 2 * owners))
    head_from = (down_rep, lax.rem(s + 2 * owners - 2, 2 * owners))
    tail_to = (down_rep, lax.rem(s + 2 * owners - 1, 2 * owners))
    tail_from = (up_rep, lax.rem(s + 1, 2 * owners))
    die_to = (r, s + 1 - 2 * core)

    my_grads = pltpu.make_async_copy(grads.at[0, pl.ds(r * half, half)], mine, mine_sem)
    my_grads.start()

    def load_own(k, rep):
        if rep == 0:
            return pltpu.make_async_copy(
                olds[k].at[pl.ds(0, WINDOW - EDGE)], main.at[k, pl.ds(EDGE, WINDOW - EDGE)], in_sem.at[k]
            )
        return pltpu.make_async_copy(olds[k].at[pl.ds(JITTER, WINDOW)], main.at[k], in_sem.at[k])

    def load_stage(k):
        rows = stage.shape[1]
        return pltpu.make_async_copy(olds[k].at[pl.ds(old_cap - rows, rows)], stage.at[k], stage_sem.at[k])

    def die_copy(k, rep):
        first = 1024 if rep == 0 else 2560
        rows = min(WINDOW, old_cap - first)
        return pltpu.make_async_remote_copy(
            olds[k].at[pl.ds(first, rows)],
            main.at[k, pl.ds(0, rows)],
            die_sem.at[0, k],
            die_sem.at[1, k],
            device_id=die_to,
            device_id_type=MESH,
        )

    def head_copy(k):
        return pltpu.make_async_remote_copy(
            edge.at[k],
            main.at[k, pl.ds(0, EDGE)],
            head_sem.at[0, k],
            head_sem.at[1, k],
            device_id=head_to,
            device_id_type=MESH,
        )

    def tail_copy(k, rep):
        first, rows = (3072, JITTER) if rep == 0 else (1536, EDGE)
        return pltpu.make_async_remote_copy(
            olds[k].at[pl.ds(0, rows)],
            alt.at[k, pl.ds(first, rows)],
            tail_sem.at[0, k],
            tail_sem.at[1, k],
            device_id=tail_to,
            device_id_type=MESH,
        )

    def grad_copy(c):
        first = pl.multiple_of(c * size, 16)
        return pltpu.make_async_remote_copy(
            grads.at[0, pl.ds(pl.multiple_of((1 - r) * half + first, 16), size)],
            theirs.at[pl.ds(first, size)],
            grad_send.at[c],
            grad_recv.at[c],
            device_id=other,
            device_id_type=MESH,
        )

    def wts_copy(c):
        first = pl.multiple_of(c * size, 16)
        return pltpu.make_async_remote_copy(
            wts.at[pl.ds(first, size)],
            out_w.at[pl.ds(pl.multiple_of(r * half + first, 16), size)],
            wts_send.at[c],
            wts_recv.at[c],
            device_id=other,
            device_id_type=MESH,
        )

    def wts_arrival(c):
        first = pl.multiple_of(c * size, 16)
        return pltpu.make_async_remote_copy(
            wts.at[pl.ds(first, size)],
            out_w.at[pl.ds(pl.multiple_of((1 - r) * half + first, 16), size)],
            wts_send.at[c],
            wts_recv.at[c],
            device_id=other,
            device_id_type=MESH,
        )

    def own_copy(c):
        first = pl.multiple_of(c * size, 16)
        return pltpu.make_async_copy(
            wts.at[pl.ds(first, size)],
            out_w.at[pl.ds(pl.multiple_of(r * half + first, 16), size)],
            own_sem.at[c],
        )

    def res_copy(k, c):
        first = pl.multiple_of(c * size, 16)
        return pltpu.make_async_copy(
            res.at[k, pl.ds(first, size)], outs[k].at[pl.ds(first, size)], res_sem.at[k, c]
        )

    for rep in (0, 1):

        @pl.when(even & (r == rep))
        def _():
            for k in range(3):
                load_own(k, rep).start()

    @pl.when(sends_head)
    def _():
        for k in range(3):
            load_stage(k).start()

    barrier = pltpu.get_barrier_semaphore()
    pl.semaphore_signal(barrier, inc=1, device_id=other, device_id_type=MESH)

    @pl.when(odd)
    def _():
        pl.semaphore_signal(barrier, inc=1, device_id=die_to, device_id_type=MESH)

    @pl.when(gets_head)
    def _():
        pl.semaphore_signal(barrier, inc=1, device_id=head_from, device_id_type=MESH)

    @pl.when(gets_tail)
    def _():
        pl.semaphore_signal(barrier, inc=1, device_id=tail_from, device_id_type=MESH)

    targets = 1 + even.astype(jnp.int32) + sends_head.astype(jnp.int32) + sends_tail.astype(jnp.int32)
    pl.semaphore_wait(barrier, targets)

    for rep, cond in ((0, sends_short), (1, sends_long)):

        @pl.when(cond)
        def _():
            for k in range(3):
                tail_copy(k, rep).start()

    @pl.loop(0, CHUNKS)
    def _(c):
        grad_copy(c).start()

    for rep in (0, 1):

        @pl.when(even & (r == rep))
        def _():
            for k in range(3):
                die_copy(k, rep).start()

    @pl.when(sends_head)
    def _():
        begin = within(old_off[o + 1] - old_off[o] - (old_cap - stage.shape[1]) - EDGE)
        for k in range(3):
            load_stage(k).wait()
        for k in range(3):

            @pl.loop(0, EDGE // SUB)
            def _(j):
                edge[k, pl.ds(pl.multiple_of(j * SUB, SUB), SUB), :] = stage[k, pl.ds(begin + j * SUB, SUB), :]

            head_copy(k).start()

    for rep in (0, 1):

        @pl.when(even & (r == rep))
        def _():
            for k in range(3):
                load_own(k, rep).wait()

        @pl.when(odd & (r == rep))
        def _():
            for k in range(3):
                die_copy(k, rep).wait_recv()

    @pl.when(gets_head)
    def _():
        for k in range(3):
            head_copy(k).wait_recv()

    for rep, cond in ((0, gets_short), (1, gets_long)):

        @pl.when(cond)
        def _():
            for k in range(3):
                tail_copy(k, rep).wait_recv()

    my_grads.wait()

    start = within(new_off[s] - old_off[o] + EDGE - 2 * EDGE * core)
    edge_start = within(new_off[s] - old_off[o + 1] + 2 * half)
    split = jnp.where(even, new_off[s + 1], old_off[o + 1])
    flat = new_off[s] + r * half
    stop = new_off[s + 1]

    @pl.loop(0, CHUNKS)
    def _(c):
        grad_copy(c).wait_recv()

        @pl.loop(0, size // SUB)
        def _(j):
            at = c * size + j * SUB
            rows = pl.ds(pl.multiple_of(at, SUB), SUB)
            row = flat + at + lax.broadcasted_iota(jnp.int32, (SUB, 128), 0)
            near = row < split
            keep = row < stop
            master, first, second = [
                jnp.where(near, main[k, pl.ds(start + at, SUB), :], alt[k, pl.ds(edge_start + at, SUB), :])
                for k in range(3)
            ]
            total = mine[rows, :] + theirs[rows, :]
            first_n = 0.9 * first + 0.1 * total
            second_n = 0.95 * second + 0.05 * total * total
            first_hat = first_n / (1.0 - 0.9**STEP)
            second_hat = second_n / (1.0 - 0.95**STEP)
            master_n = master - 0.02 * (first_hat / (jnp.sqrt(second_hat) + 1e-08) + 0.1 * master)
            master_n = jnp.where(keep, master_n, 0.0)
            res[0, rows, :] = master_n
            res[1, rows, :] = jnp.where(keep, first_n, 0.0)
            res[2, rows, :] = jnp.where(keep, second_n, 0.0)
            wts[rows, :] = master_n.astype(jnp.bfloat16)

        wts_copy(c).start()
        own_copy(c).start()
        for k in range(3):
            res_copy(k, c).start()

    for rep in (0, 1):

        @pl.when(even & (r == rep))
        def _():
            for k in range(3):
                die_copy(k, rep).wait_send()

    @pl.when(sends_head)
    def _():
        for k in range(3):
            head_copy(k).wait_send()

    for rep, cond in ((0, sends_short), (1, sends_long)):

        @pl.when(cond)
        def _():
            for k in range(3):
                tail_copy(k, rep).wait_send()

    @pl.loop(0, CHUNKS)
    def _(c):
        grad_copy(c).wait_send()
        for k in range(3):
            res_copy(k, c).wait()
        own_copy(c).wait()
        wts_copy(c).wait_send()
        wts_arrival(c).wait_recv()


def local(old_master, old_first, old_second, grad_parts, old_offsets, new_offsets):
    new_cap, lanes = grad_parts.shape[1:]
    half = new_cap // 2
    smem = pl.BlockSpec(memory_space=pltpu.SMEM)
    hbm = pl.BlockSpec(memory_space=pl.ANY)
    state = jax.ShapeDtypeStruct((half, lanes), jnp.float32)
    dma = pltpu.SemaphoreType.DMA
    master, first, second, weights = pl.pallas_call(
        kernel,
        out_shape=(state, state, state, jax.ShapeDtypeStruct((new_cap, lanes), jnp.bfloat16)),
        in_specs=[smem, smem, hbm, hbm, hbm, hbm],
        out_specs=(hbm, hbm, hbm, hbm),
        scratch_shapes=[
            pltpu.VMEM((3, WINDOW, lanes), jnp.float32),
            pltpu.VMEM((3, WINDOW, lanes), jnp.float32),
            pltpu.VMEM((3, 3 * EDGE, lanes), jnp.float32),
            pltpu.VMEM((3, EDGE, lanes), jnp.float32),
            pltpu.VMEM((half, lanes), jnp.float32),
            pltpu.VMEM((half, lanes), jnp.float32),
            pltpu.VMEM((3, half, lanes), jnp.float32),
            pltpu.VMEM((half, lanes), jnp.bfloat16),
            dma((3,)),
            dma,
            dma((3,)),
            dma((2, 3)),
            dma((2, 3)),
            dma((2, 3)),
            dma((CHUNKS,)),
            dma((CHUNKS,)),
            dma((CHUNKS,)),
            dma((CHUNKS,)),
            dma((3, CHUNKS)),
            dma((CHUNKS,)),
        ],
        compiler_params=pltpu.CompilerParams(
            collective_id=0, has_side_effects=True, vmem_limit_bytes=48 * 1024 * 1024
        ),
        name="move_and_update",
    )(old_offsets, new_offsets, old_master, old_first, old_second, grad_parts)
    return (master[None, None], first[None, None], second[None, None], weights)


def solution(mesh):
    in_specs = (
        P("shard", None),
        P("shard", None),
        P("shard", None),
        P("rep", "shard", None),
        P(),
        P(),
    )
    out_specs = (
        P("shard", "rep", None, None),
        P("shard", "rep", None, None),
        P("shard", "rep", None, None),
        P("shard", None),
    )
    return jax.shard_map(local, mesh=mesh, in_specs=in_specs, out_specs=out_specs, check_vma=False)
```

time: 274 us -> 91.8 us (0.34)
  waiting for transfers between devices: 129 us -> 0 us
  Pallas kernels: 0 us -> 84.5 us
  starting transfers between devices: 49.9 us -> 0 us
  blocking collectives: 33 us -> 0 us
  other arithmetic: 31.3 us -> 0 us
  between operations: 22.7 us -> 0.65 us
    ppermute x9 -> x0, waiting for transfers between devices: 129 us -> none  [from_behind(): return lax.ppermute(x, axis, pairs)]
    pallas_call x0 -> x1, Pallas kernels: none -> 84.5 us  [local(): pl.pallas_call(kernel, out_shape=(state, state, state, jax.ShapeDtypeStru...]
    ppermute x9 -> x0, starting transfers between devices: 49.9 us -> none  [from_behind(): return lax.ppermute(x, axis, pairs)]
    all_gather x1 -> x0, blocking collectives: 33 us -> none  [local(): lax.all_gather(master_n.astype(jnp.bfloat16), 'rep', axis=0, tiled=True)]
    select_n x1 -> x0, other arithmetic: 9.56 us -> none  [rows_for(): jnp.where(keep[:, None], lax.dynamic_slice_in_dim(block, start, extent, 0...]
    concatenate x1 -> x0, other arithmetic: 7.82 us -> none  [local(): jnp.concatenate([jnp.zeros((new_cap, lanes), jnp.float32), state, jnp.zer...]
    and x3 -> x0, other arithmetic: 6.6 us -> none  [rows_for(): (flat_rows < new_offsets[target + 1]) & (flat_rows >= old_start)]
    unnamed x7 -> x10, local copies, waits for them, and re-layouts: 0.97 us -> 6.25 us
  transfers between devices with their start and end apart: 10 -> 0, of which waited for: 5 -> 0; matrix products, arithmetic and copies ran while one was open for 1% -> 0% of each run, Pallas kernels for 0% -> 0%
where the time goes in v1:
time: 91.8 us; the launch traced here: 91.4 us
  Pallas kernels  84.5 us (92%)
  local copies, waits for them, and re-layouts  6.25 us (7%)
    pallas_call x1, Pallas kernels, local(): pl.pallas_call(kernel, out_shape=(state, state, state, jax.ShapeDtypeStru...  84.5 us
    unnamed x10, local copies, waits for them, and re-layouts  6.25 us

profile of v1, /device:TPU:8, one launch (start us, length us, event | category | flops | bytes accessed | tf_op | source)
XLA Modules:
  0.0 91.4 jit_solution(17294648957341157884)
XLA Ops:
  0.6 0.0 copy-start
  0.6 1.4 %copy-done = f32[1,3072,128]{2,1,0:T(8,128)S(1)} copy-done((f32[1,3072,128]{2,1,0:T(8,128)S(1)}, f32[1,3072,128]{2,1,0:T(8,128)}, u32[]{:S(2)}) %copy-start) | copy-done | bytes 1572888
  2.0 0.0 copy-start.1
  2.0 0.7 copy-done.1
  2.7 0.0 copy-start.2
  2.7 0.7 copy-done.2
  3.4 84.5 %move_and_update.1 = (f32[1536,128]{1,0:T(8,128)S(1)}, f32[1536,128]{1,0:T(8,128)S(1)}, f32[1536,128]{1,0:T(8,128)S(1)}, bf16[3072,128]{1,0:T(8,128)(2,1)S(1)}) custom-call(s32[65]{0:T(128)S(1)} %copy-done.2, s32[129]{0:T(256)S(1)} %copy-done.1, f32[5120,128]{1,0:T(8,128)} %old_m.1, f32[5120,128]{1,0:T(8,128)} %old_f.1, f32[5120,128]{1,0:T(8,128)} %old_s.1, ...), custom_call_target="tpu_custom_call" | custom-call | tf_op jit(solution)/shard_map/move_and_update/pallas_call | solution.py:340
  87.9 0.9 copy.14
  88.7 0.9 copy.15
  89.6 0.9 copy.16
  90.5 0.9 copy.17
Async XLA Ops:
  0.6 1.4 %copy-start = (f32[1,3072,128]{2,1,0:T(8,128)S(1)}, f32[1,3072,128]{2,1,0:T(8,128)}, u32[]{:S(2)}) copy-start(f32[1,3072,128]{2,1,0:T(8,128)} %grads.1) | copy-start | bytes 4718596
  2.0 0.7 copy-start.1
  2.7 0.7 copy-start.2

commit v2 on v1

--- a/solution.py
+++ b/solution.py
@@ -21,8 +21,8 @@
 
 
 def kernel(
-    old_off,
-    new_off,
+    old_off_in,
+    new_off_in,
     old_m,
     old_f,
     old_s,
@@ -31,20 +31,26 @@
     out_f,
     out_s,
     out_w,
+    old_off,
+    new_off,
     main,
     alt,
+    relay,
     stage,
     edge,
     mine,
     theirs,
     res,
     wts,
+    off_sem,
     in_sem,
     mine_sem,
     stage_sem,
     die_sem,
     head_sem,
     tail_sem,
+    head_relay_sem,
+    tail_relay_sem,
     grad_send,
     grad_recv,
     wts_send,
@@ -66,22 +72,39 @@
     odd = core == 1
     other = (1 - r, s)
 
+    x = o % 4
+
     up_rep = jnp.where(o % 16 == 15, 1 - r, r)
     down_rep = jnp.where(o % 16 == 0, 1 - r, r)
     sends_head = even & (up_rep == 0) & (o < owners - 1)
     gets_head = even & (r == 0) & (o > 0)
     sends_tail = even & (o > 0)
-    sends_short = sends_tail & (down_rep == 0)
-    sends_long = sends_tail & (down_rep == 1)
     gets_tail = odd & (o < owners - 1)
-    gets_short = gets_tail & (r == 0)
-    gets_long = gets_tail & (r == 1)
-    head_to = (up_rep, lax.rem(s + 2, 2 * owners))
-    head_from = (down_rep, lax.rem(s + 2 * owners - 2, 2 * owners))
-    tail_to = (down_rep, lax.rem(s + 2 * owners - 1, 2 * owners))
-    tail_from = (up_rep, lax.rem(s + 1, 2 * owners))
+    count = 2 * owners
+    head_to = (up_rep, lax.rem(s + 2, count))
+    head_from = (down_rep, lax.rem(s + count - 2, count))
+    tail_to = (down_rep, lax.rem(s + count - 1, count))
+    tail_from = (up_rep, lax.rem(s + 1, count))
     die_to = (r, s + 1 - 2 * core)
 
+    z_lo = (o // 4) % 4
+    head_wraps = sends_head & (x == 3)
+    head_unwraps = gets_head & (x == 0)
+    tail_wraps = sends_tail & (x == 0)
+    tail_unwraps = gets_tail & (x == 3)
+    head_source = s - 1 + 2 * (3 - x)
+    head_rep = jnp.where(z_lo == 3, 1 - r, r)
+    relays_head = odd & (x < 3) & (head_rep == 0) & (head_source < count - 2)
+    tail_source = s - 1 - 2 * x
+    tail_rep = jnp.where(z_lo == 0, 1 - r, r)
+    relays_tail = odd & (x > 0) & (tail_source > 0)
+
+    offsets = (
+        pltpu.make_async_copy(old_off_in, old_off, off_sem.at[0]),
+        pltpu.make_async_copy(new_off_in, new_off, off_sem.at[1]),
+    )
+    for copy in offsets:
+        copy.start()
     my_grads = pltpu.make_async_copy(grads.at[0, pl.ds(r * half, half)], mine, mine_sem)
     my_grads.start()
 
@@ -108,26 +131,52 @@
             device_id_type=MESH,
         )
 
-    def head_copy(k):
-        return pltpu.make_async_remote_copy(
-            edge.at[k],
-            main.at[k, pl.ds(0, EDGE)],
-            head_sem.at[0, k],
-            head_sem.at[1, k],
-            device_id=head_to,
-            device_id_type=MESH,
-        )
-
-    def tail_copy(k, rep):
-        first, rows = (3072, JITTER) if rep == 0 else (1536, EDGE)
-        return pltpu.make_async_remote_copy(
-            olds[k].at[pl.ds(0, rows)],
-            alt.at[k, pl.ds(first, rows)],
-            tail_sem.at[0, k],
-            tail_sem.at[1, k],
-            device_id=tail_to,
-            device_id_type=MESH,
-        )
+    def send(src, dst, sems, to):
+        return pltpu.make_async_remote_copy(src, dst, sems[0], sems[1], device_id=to, device_id_type=MESH)
+
+    quarter = EDGE // 4
+
+    def head_copy(k, part=None):
+        rows = pl.ds(0, EDGE) if part is None else pl.ds(part * quarter, quarter)
+        at = 0 if part is None else part
+        sems = (head_sem.at[0, at, k], head_sem.at[1, at, k])
+        return send(edge.at[k, rows], main.at[k, rows], sems, head_to)
+
+    def head_relay_in(k, part):
+        rows = pl.ds(part * quarter, quarter)
+        sems = (head_sem.at[0, part, k], head_relay_sem.at[0, k])
+        return send(edge.at[k, rows], relay.at[0, k], sems, (r, s - 2 * (3 - part) + 1))
+
+    def head_relay_out(k, part):
+        rows = pl.ds(part * quarter, quarter)
+        sems = (head_relay_sem.at[1, k], head_sem.at[1, part, k])
+        return send(relay.at[0, k], main.at[k, rows], sems, (head_rep, lax.rem(head_source + 2, count)))
+
+    def tail_place(rep):
+        return (3072, JITTER) if rep == 0 else (1536, EDGE)
+
+    def tail_copy(k, rep, part=None):
+        first, rows = tail_place(rep)
+        begin = 0
+        if part is not None:
+            rows //= 4
+            begin = part * rows
+        at = 0 if part is None else part
+        sems = (tail_sem.at[0, at, k], tail_sem.at[1, at, k])
+        return send(olds[k].at[pl.ds(begin, rows)], alt.at[k, pl.ds(first + begin, rows)], sems, tail_to)
+
+    def tail_relay_in(k, rep, part):
+        rows = tail_place(rep)[1] // 4
+        sems = (tail_sem.at[0, part, k], tail_relay_sem.at[0, k])
+        to = (r, lax.rem(s + 2 * part + 1, count))
+        return send(olds[k].at[pl.ds(part * rows, rows)], relay.at[1, k, pl.ds(0, rows)], sems, to)
+
+    def tail_relay_out(k, rep, part):
+        first, rows = tail_place(rep)
+        rows //= 4
+        sems = (tail_relay_sem.at[1, k], tail_sem.at[1, part, k])
+        to = (tail_rep, lax.rem(tail_source + count - 1, count))
+        return send(relay.at[1, k, pl.ds(0, rows)], alt.at[k, pl.ds(first + part * rows, rows)], sems, to)
 
     def grad_copy(c):
         first = pl.multiple_of(c * size, 16)
@@ -199,19 +248,57 @@
     def _():
         pl.semaphore_signal(barrier, inc=1, device_id=head_from, device_id_type=MESH)
 
+    @pl.when(head_unwraps)
+    def _():
+        for part in (0, 1, 2):
+            at = lax.rem(s + count - 2 - 2 * (3 - part) + 1, count)
+            pl.semaphore_signal(barrier, inc=1, device_id=(down_rep, at), device_id_type=MESH)
+
     @pl.when(gets_tail)
     def _():
         pl.semaphore_signal(barrier, inc=1, device_id=tail_from, device_id_type=MESH)
 
-    targets = 1 + even.astype(jnp.int32) + sends_head.astype(jnp.int32) + sends_tail.astype(jnp.int32)
+    @pl.when(tail_unwraps)
+    def _():
+        for part in (1, 2, 3):
+            at = lax.rem(s + 2 * part + 2, count)
+            pl.semaphore_signal(barrier, inc=1, device_id=(up_rep, at), device_id_type=MESH)
+
+    @pl.when(relays_head)
+    def _():
+        pl.semaphore_signal(barrier, inc=1, device_id=(r, lax.rem(head_source, count)), device_id_type=MESH)
+
+    @pl.when(relays_tail)
+    def _():
+        pl.semaphore_signal(barrier, inc=1, device_id=(r, lax.rem(tail_source + count, count)), device_id_type=MESH)
+
+    targets = 1
+    for cond, more in (
+        (even, 1),
+        (sends_head, 1),
+        (head_wraps, 3),
+        (sends_tail, 1),
+        (tail_wraps, 3),
+        (relays_head, 1),
+        (relays_tail, 1),
+    ):
+        targets = targets + more * cond.astype(jnp.int32)
     pl.semaphore_wait(barrier, targets)
 
-    for rep, cond in ((0, sends_short), (1, sends_long)):
-
-        @pl.when(cond)
+    for rep in (0, 1):
+
+        @pl.when(sends_tail & (down_rep == rep) & (x > 0))
         def _():
             for k in range(3):
                 tail_copy(k, rep).start()
+
+        @pl.when(tail_wraps & (down_rep == rep))
+        def _():
+            for part in (1, 2, 3):
+                for k in range(3):
+                    tail_relay_in(k, rep, part).start()
+            for k in range(3):
+                tail_copy(k, rep, 0).start()
 
     @pl.loop(0, CHUNKS)
     def _(c):
@@ -224,6 +311,9 @@
             for k in range(3):
                 die_copy(k, rep).start()
 
+    for copy in offsets:
+        copy.wait()
+
     @pl.when(sends_head)
     def _():
         begin = within(old_off[o + 1] - old_off[o] - (old_cap - stage.shape[1]) - EDGE)
@@ -235,7 +325,32 @@
             def _(j):
                 edge[k, pl.ds(pl.multiple_of(j * SUB, SUB), SUB), :] = stage[k, pl.ds(begin + j * SUB, SUB), :]
 
-            head_copy(k).start()
+            @pl.when(x < 3)
+            def _():
+                head_copy(k).start()
+
+            @pl.when(x == 3)
+            def _():
+                for part in (0, 1, 2):
+                    head_relay_in(k, part).start()
+                head_copy(k, 3).start()
+
+    for rep in (0, 1):
+        for part in (1, 2, 3):
+
+            @pl.when(relays_tail & (tail_rep == rep) & (x == part))
+            def _():
+                for k in range(3):
+                    tail_relay_in(k, rep, part).wait_recv()
+                    tail_relay_out(k, rep, part).start()
+
+    for part in (0, 1, 2):
+
+        @pl.when(relays_head & (x == part))
+        def _():
+            for k in range(3):
+                head_relay_in(k, part).wait_recv()
+                head_relay_out(k, part).start()
 
     for rep in (0, 1):
 
@@ -249,17 +364,29 @@
             for k in range(3):
                 die_copy(k, rep).wait_recv()
 
-    @pl.when(gets_head)
+    @pl.when(gets_head & (x > 0))
     def _():
         for k in range(3):
             head_copy(k).wait_recv()
 
-    for rep, cond in ((0, gets_short), (1, gets_long)):
-
-        @pl.when(cond)
+    @pl.when(head_unwraps)
+    def _():
+        for part in range(4):
+            for k in range(3):
+                head_copy(k, part).wait_recv()
+
+    for rep in (0, 1):
+
+        @pl.when(gets_tail & (r == rep) & (x < 3))
         def _():
             for k in range(3):
                 tail_copy(k, rep).wait_recv()
+
+        @pl.when(tail_unwraps & (r == rep))
+        def _():
+            for part in range(4):
+                for k in range(3):
+                    tail_copy(k, rep, part).wait_recv()
 
     my_grads.wait()
 
@@ -308,17 +435,39 @@
             for k in range(3):
                 die_copy(k, rep).wait_send()
 
-    @pl.when(sends_head)
+    @pl.when(sends_head & (x < 3))
     def _():
         for k in range(3):
             head_copy(k).wait_send()
 
-    for rep, cond in ((0, sends_short), (1, sends_long)):
-
-        @pl.when(cond)
+    @pl.when(head_wraps)
+    def _():
+        for part in range(4):
+            for k in range(3):
+                head_copy(k, part).wait_send()
+
+    @pl.when(relays_head)
+    def _():
+        for k in range(3):
+            head_relay_out(k, 0).wait_send()
+
+    for rep in (0, 1):
+
+        @pl.when(sends_tail & (down_rep == rep) & (x > 0))
         def _():
             for k in range(3):
                 tail_copy(k, rep).wait_send()
+
+        @pl.when(tail_wraps & (down_rep == rep))
+        def _():
+            for part in range(4):
+                for k in range(3):
+                    tail_copy(k, rep, part).wait_send()
+
+        @pl.when(relays_tail & (tail_rep == rep))
+        def _():
+            for k in range(3):
+                tail_relay_out(k, rep, 0).wait_send()
 
     @pl.loop(0, CHUNKS)
     def _(c):
@@ -330,31 +479,47 @@
         wts_arrival(c).wait_recv()
 
 
+def finish(in_m, in_f, in_s, in_w, out_m, out_f, out_s, out_w, sem):
+    pairs = ((in_m, out_m), (in_f, out_f), (in_s, out_s), (in_w, out_w))
+    copies = [pltpu.make_async_copy(src, dst, sem.at[i]) for i, (src, dst) in enumerate(pairs)]
+    for copy in copies:
+        copy.start()
+    for copy in copies:
+        copy.wait()
+
+
 def local(old_master, old_first, old_second, grad_parts, old_offsets, new_offsets):
     new_cap, lanes = grad_parts.shape[1:]
     half = new_cap // 2
-    smem = pl.BlockSpec(memory_space=pltpu.SMEM)
-    hbm = pl.BlockSpec(memory_space=pl.ANY)
+    hbm = pl.BlockSpec(memory_space=pltpu.HBM)
+    free = pl.BlockSpec(memory_space=pl.ANY)
     state = jax.ShapeDtypeStruct((half, lanes), jnp.float32)
     dma = pltpu.SemaphoreType.DMA
-    master, first, second, weights = pl.pallas_call(
+    shapes = (state, state, state, jax.ShapeDtypeStruct((new_cap, lanes), jnp.bfloat16))
+    results = pl.pallas_call(
         kernel,
-        out_shape=(state, state, state, jax.ShapeDtypeStruct((new_cap, lanes), jnp.bfloat16)),
-        in_specs=[smem, smem, hbm, hbm, hbm, hbm],
-        out_specs=(hbm, hbm, hbm, hbm),
+        out_shape=shapes,
+        in_specs=[hbm] * 6,
+        out_specs=(free, free, free, free),
         scratch_shapes=[
+            pltpu.SMEM(old_offsets.shape, jnp.int32),
+            pltpu.SMEM(new_offsets.shape, jnp.int32),
             pltpu.VMEM((3, WINDOW, lanes), jnp.float32),
             pltpu.VMEM((3, WINDOW, lanes), jnp.float32),
+            pltpu.VMEM((2, 3, EDGE // 4, lanes), jnp.float32),
             pltpu.VMEM((3, 3 * EDGE, lanes), jnp.float32),
             pltpu.VMEM((3, EDGE, lanes), jnp.float32),
             pltpu.VMEM((half, lanes), jnp.float32),
             pltpu.VMEM((half, lanes), jnp.float32),
             pltpu.VMEM((3, half, lanes), jnp.float32),
             pltpu.VMEM((half, lanes), jnp.bfloat16),
+            dma((2,)),
             dma((3,)),
             dma,
             dma((3,)),
             dma((2, 3)),
+            dma((2, 4, 3)),
+            dma((2, 4, 3)),
             dma((2, 3)),
             dma((2, 3)),
             dma((CHUNKS,)),
@@ -369,6 +534,14 @@
         ),
         name="move_and_update",
     )(old_offsets, new_offsets, old_master, old_first, old_second, grad_parts)
+    master, first, second, weights = pl.pallas_call(
+        finish,
+        out_shape=shapes,
+        in_specs=[free] * 4,
+        out_specs=(hbm,) * 4,
+        scratch_shapes=[dma((4,))],
+        name="finish",
+    )(*results)
     return (master[None, None], first[None, None], second[None, None], weights)
 
 

time: 91.8 us -> 181 us (1.97)
  Pallas kernels: 84.5 us -> 174 us
    pallas_call x1 -> x2, Pallas kernels: 84.5 us -> 174 us  [the longest x1 96.4 us: local(): pl.pallas_call(finish, out_shape=shapes, in_specs=[free] * 4, out_specs=(...]
    unnamed x10 -> x14, local copies, waits for them, and re-layouts: 6.25 us -> 6.27 us
where the time goes in v2:
time: 181 us
  Pallas kernels  174 us (96%)
  local copies, waits for them, and re-layouts  6.27 us (3%)
    pallas_call x1, Pallas kernels, local(): pl.pallas_call(finish, out_shape=shapes, in_specs=[free] * 4, out_specs=(...  96.4 us
    pallas_call x1, Pallas kernels, local(): pl.pallas_call(kernel, out_shape=shapes, in_specs=[hbm] * 6, out_specs=(f...  77.7 us
    unnamed x14, local copies, waits for them, and re-layouts  6.27 us

profile of v2, /device:TPU:8, one launch (start us, length us, event | category | flops | bytes accessed | tf_op | source)
XLA Modules:
  0.0 181.1 jit_solution(12312526991395623198)
XLA Ops:
  0.6 0.0 copy-start
  0.6 1.4 copy-done
  2.0 0.0 copy-start.5
  2.0 0.7 copy-done.5
  2.7 0.0 copy-start.6
  2.7 0.7 copy-done.6
  3.4 77.7 %move_and_update.1 = (f32[1536,128]{1,0:T(8,128)S(1)}, f32[1536,128]{1,0:T(8,128)S(1)}, f32[1536,128]{1,0:T(8,128)S(1)}, bf16[3072,128]{1,0:T(8,128)(2,1)S(1)}) custom-call(s32[65]{0:T(128)S(1)} %copy-done.6, s32[129]{0:T(256)S(1)} %copy-done.5, f32[5120,128]{1,0:T(8,128)} %old_m.1, f32[5120,128]{1,0:T(8,128)} %old_f.1, f32[5120,128]{1,0:T(8,128)} %old_s.1, ...), custom_call_target="tpu_custom_call" | custom-call | tf_op jit(solution)/shard_map/move_and_update/pallas_call | solution.py:499
  81.1 0.0 copy-start.1
  81.1 0.9 copy-done.1
  82.0 0.0 copy-start.2
  82.0 0.9 copy-done.2
  82.9 0.0 copy-start.3
  82.9 0.9 copy-done.3
  83.8 0.0 copy-start.4
  83.8 0.9 copy-done.4
  84.6 96.4 %finish.1 = (f32[1536,128]{1,0:T(8,128)}, f32[1536,128]{1,0:T(8,128)}, f32[1536,128]{1,0:T(8,128)}, bf16[3072,128]{1,0:T(8,128)(2,1)}) custom-call(f32[1536,128]{1,0:T(8,128)} %copy-done.1, f32[1536,128]{1,0:T(8,128)} %copy-done.2, f32[1536,128]{1,0:T(8,128)} %copy-done.3, bf16[3072,128]{1,0:T(8,128)(2,1)} %copy-done.4), custom_call_target="tpu_custom_call" | custom-call | tf_op jit(solution)/shard_map/finish/pallas_call | solution.py:537
Async XLA Ops:
  0.6 1.4 copy-start
  2.0 0.7 copy-start.5
  2.7 0.7 copy-start.6
  81.1 0.9 copy-start.1
  82.0 0.9 copy-start.2
  82.9 0.9 copy-start.3
  83.8 0.9 copy-start.4

commit v3 on v2

--- a/solution.py
+++ b/solution.py
@@ -88,16 +88,20 @@
     die_to = (r, s + 1 - 2 * core)
 
     z_lo = (o // 4) % 4
+    turn_up = jnp.where(z_lo == 3, 32, 0)
+    turn_down = jnp.where(z_lo == 0, 32, 0)
     head_wraps = sends_head & (x == 3)
     head_unwraps = gets_head & (x == 0)
     tail_wraps = sends_tail & (x == 0)
     tail_unwraps = gets_tail & (x == 3)
-    head_source = s - 1 + 2 * (3 - x)
+    head_source = s - 1 + 2 * (3 - x) - turn_up
     head_rep = jnp.where(z_lo == 3, 1 - r, r)
-    relays_head = odd & (x < 3) & (head_rep == 0) & (head_source < count - 2)
-    tail_source = s - 1 - 2 * x
+    relays_head = odd & (head_rep == 0) & (head_source >= 0)
+    tail_source = s - 1 - 2 * x + turn_down
     tail_rep = jnp.where(z_lo == 0, 1 - r, r)
-    relays_tail = odd & (x > 0) & (tail_source > 0)
+    relays_tail = odd & (tail_source < count)
+    head_relays = s + jnp.where(z_lo == 0, 24, -8) + 1
+    tail_relays = s + jnp.where(z_lo == 3, -24, 8) - 6
 
     offsets = (
         pltpu.make_async_copy(old_off_in, old_off, off_sem.at[0]),
@@ -145,7 +149,8 @@
     def head_relay_in(k, part):
         rows = pl.ds(part * quarter, quarter)
         sems = (head_sem.at[0, part, k], head_relay_sem.at[0, k])
-        return send(edge.at[k, rows], relay.at[0, k], sems, (r, s - 2 * (3 - part) + 1))
+        to = (r, lax.rem(s - 2 * (3 - part) + 1 + turn_up + count, count))
+        return send(edge.at[k, rows], relay.at[0, k], sems, to)
 
     def head_relay_out(k, part):
         rows = pl.ds(part * quarter, quarter)
@@ -168,7 +173,7 @@
     def tail_relay_in(k, rep, part):
         rows = tail_place(rep)[1] // 4
         sems = (tail_sem.at[0, part, k], tail_relay_sem.at[0, k])
-        to = (r, lax.rem(s + 2 * part + 1, count))
+        to = (r, lax.rem(s + 2 * part + 1 - turn_down + count, count))
         return send(olds[k].at[pl.ds(part * rows, rows)], relay.at[1, k, pl.ds(0, rows)], sems, to)
 
     def tail_relay_out(k, rep, part):
@@ -244,33 +249,33 @@
     def _():
         pl.semaphore_signal(barrier, inc=1, device_id=die_to, device_id_type=MESH)
 
-    @pl.when(gets_head)
+    @pl.when(gets_head & (x > 0))
     def _():
         pl.semaphore_signal(barrier, inc=1, device_id=head_from, device_id_type=MESH)
 
     @pl.when(head_unwraps)
     def _():
-        for part in (0, 1, 2):
-            at = lax.rem(s + count - 2 - 2 * (3 - part) + 1, count)
+        for part in range(4):
+            at = lax.rem(head_relays + 2 * part + count, count)
             pl.semaphore_signal(barrier, inc=1, device_id=(down_rep, at), device_id_type=MESH)
 
-    @pl.when(gets_tail)
+    @pl.when(gets_tail & (x < 3))
     def _():
         pl.semaphore_signal(barrier, inc=1, device_id=tail_from, device_id_type=MESH)
 
     @pl.when(tail_unwraps)
     def _():
-        for part in (1, 2, 3):
-            at = lax.rem(s + 2 * part + 2, count)
+        for part in range(4):
+            at = lax.rem(tail_relays + 2 * part + count, count)
             pl.semaphore_signal(barrier, inc=1, device_id=(up_rep, at), device_id_type=MESH)
 
     @pl.when(relays_head)
     def _():
-        pl.semaphore_signal(barrier, inc=1, device_id=(r, lax.rem(head_source, count)), device_id_type=MESH)
+        pl.semaphore_signal(barrier, inc=1, device_id=(r, lax.rem(head_source + count, count)), device_id_type=MESH)
 
     @pl.when(relays_tail)
     def _():
-        pl.semaphore_signal(barrier, inc=1, device_id=(r, lax.rem(tail_source + count, count)), device_id_type=MESH)
+        pl.semaphore_signal(barrier, inc=1, device_id=(r, lax.rem(tail_source, count)), device_id_type=MESH)
 
     targets = 1
     for cond, more in (
@@ -294,11 +299,9 @@
 
         @pl.when(tail_wraps & (down_rep == rep))
         def _():
-            for part in (1, 2, 3):
+            for part in range(4):
                 for k in range(3):
                     tail_relay_in(k, rep, part).start()
-            for k in range(3):
-                tail_copy(k, rep, 0).start()
 
     @pl.loop(0, CHUNKS)
     def _(c):
@@ -331,12 +334,11 @@
 
             @pl.when(x == 3)
             def _():
-                for part in (0, 1, 2):
+                for part in range(4):
                     head_relay_in(k, part).start()
-                head_copy(k, 3).start()
-
-    for rep in (0, 1):
-        for part in (1, 2, 3):
+
+    for rep in (0, 1):
+        for part in range(4):
 
             @pl.when(relays_tail & (tail_rep == rep) & (x == part))
             def _():
@@ -344,7 +346,7 @@
                     tail_relay_in(k, rep, part).wait_recv()
                     tail_relay_out(k, rep, part).start()
 
-    for part in (0, 1, 2):
+    for part in range(4):
 
         @pl.when(relays_head & (x == part))
         def _():
@@ -530,14 +532,14 @@
             dma((CHUNKS,)),
         ],
         compiler_params=pltpu.CompilerParams(
-            collective_id=0, has_side_effects=True, vmem_limit_bytes=48 * 1024 * 1024
+            collective_id=0, has_side_effects=True, vmem_limit_bytes=50 * 1024 * 1024
         ),
         name="move_and_update",
     )(old_offsets, new_offsets, old_master, old_first, old_second, grad_parts)
     master, first, second, weights = pl.pallas_call(
         finish,
         out_shape=shapes,
-        in_specs=[free] * 4,
+        in_specs=[pl.BlockSpec(memory_space=pltpu.VMEM)] * 4,
         out_specs=(hbm,) * 4,
         scratch_shapes=[dma((4,))],
         name="finish",

time: 181 us -> 82.5 us (0.46)
  Pallas kernels: 174 us -> 76.8 us
    pallas_call x1, Pallas kernels: 96.4 us -> 3.53 us  [local(): pl.pallas_call(finish, out_shape=shapes, in_specs=[pl.BlockSpec(memory_sp...]
    pallas_call x1, Pallas kernels: 77.7 us -> 73.3 us  [local(): pl.pallas_call(kernel, out_shape=shapes, in_specs=[hbm] * 6, out_specs=(f...]
    unnamed x14 -> x12, local copies, waits for them, and re-layouts: 6.27 us -> 4.87 us
where the time goes in v3:
time: 82.5 us; the launch traced here: 82.4 us
  Pallas kernels  76.8 us (93%)
  local copies, waits for them, and re-layouts  4.87 us (6%)
    pallas_call x1, Pallas kernels, local(): pl.pallas_call(kernel, out_shape=shapes, in_specs=[hbm] * 6, out_specs=(f...  73.3 us
    unnamed x12, local copies, waits for them, and re-layouts  4.87 us
    pallas_call x1, Pallas kernels, local(): pl.pallas_call(finish, out_shape=shapes, in_specs=[pl.BlockSpec(memory_sp...  3.53 us

profile of v3, /device:TPU:8, one launch (start us, length us, event | category | flops | bytes accessed | tf_op | source)
XLA Modules:
  0.0 82.4 jit_solution(12380342743033727758)
XLA Ops:
  0.6 0.0 copy-start.4
  0.6 0.7 copy-done.4
  1.3 0.0 copy-start.5
  1.3 0.7 copy-done.5
  2.0 73.3 %move_and_update.1 = (f32[1536,128]{1,0:T(8,128)S(1)}, f32[1536,128]{1,0:T(8,128)S(1)}, f32[1536,128]{1,0:T(8,128)S(1)}, bf16[3072,128]{1,0:T(8,128)(2,1)S(1)}) custom-call(s32[65]{0:T(128)S(1)} %copy-done.5, s32[129]{0:T(256)S(1)} %copy-done.4, f32[5120,128]{1,0:T(8,128)} %old_m.1, f32[5120,128]{1,0:T(8,128)} %old_f.1, f32[5120,128]{1,0:T(8,128)} %old_s.1, ...), custom_call_target="tpu_custom_call" | custom-call | tf_op jit(solution)/shard_map/move_and_update/pallas_call | solution.py:501
  75.3 0.0 copy-start
  75.3 0.9 %copy-done = f32[1536,128]{1,0:T(8,128)} copy-done((f32[1536,128]{1,0:T(8,128)}, f32[1536,128]{1,0:T(8,128)S(1)}, u32[]{:S(2)}) %copy-start) | copy-done | bytes 786456
  76.2 0.0 copy-start.1
  76.2 0.9 %copy-done.1 = f32[1536,128]{1,0:T(8,128)} copy-done((f32[1536,128]{1,0:T(8,128)}, f32[1536,128]{1,0:T(8,128)S(1)}, u32[]{:S(2)}) %copy-start.1) | copy-done | bytes 786456
  77.1 0.0 copy-start.2
  77.1 0.9 %copy-done.2 = f32[1536,128]{1,0:T(8,128)} copy-done((f32[1536,128]{1,0:T(8,128)}, f32[1536,128]{1,0:T(8,128)S(1)}, u32[]{:S(2)}) %copy-start.2) | copy-done | bytes 786456
  78.0 0.0 copy-start.3
  78.0 0.9 %copy-done.3 = bf16[3072,128]{1,0:T(8,128)(2,1)} copy-done((bf16[3072,128]{1,0:T(8,128)(2,1)}, bf16[3072,128]{1,0:T(8,128)(2,1)S(1)}, u32[]{:S(2)}) %copy-start.3) | copy-done | bytes 786456
  78.8 3.5 %finish.1 = (f32[1536,128]{1,0:T(8,128)}, f32[1536,128]{1,0:T(8,128)}, f32[1536,128]{1,0:T(8,128)}, bf16[3072,128]{1,0:T(8,128)(2,1)}) custom-call(f32[1536,128]{1,0:T(8,128)} %copy-done, f32[1536,128]{1,0:T(8,128)} %copy-done.1, f32[1536,128]{1,0:T(8,128)} %copy-done.2, bf16[3072,128]{1,0:T(8,128)(2,1)} %copy-done.3), custom_call_target="tpu_custom_call" | custom-call | tf_op jit(solution)/shard_map/finish/pallas_call | solution.py:539
Async XLA Ops:
  0.6 0.7 copy-start.4
  1.3 0.7 copy-start.5
  75.3 0.9 %copy-start = (f32[1536,128]{1,0:T(8,128)}, f32[1536,128]{1,0:T(8,128)S(1)}, u32[]{:S(2)}) copy-start(f32[1536,128]{1,0:T(8,128)S(1)} %get-tuple-element.12.in_m) | copy-start | bytes 2359300
  76.2 0.9 %copy-start.1 = (f32[1536,128]{1,0:T(8,128)}, f32[1536,128]{1,0:T(8,128)S(1)}, u32[]{:S(2)}) copy-start(f32[1536,128]{1,0:T(8,128)S(1)} %get-tuple-element.13.in_f) | copy-start | bytes 2359300
  77.1 0.9 %copy-start.2 = (f32[1536,128]{1,0:T(8,128)}, f32[1536,128]{1,0:T(8,128)S(1)}, u32[]{:S(2)}) copy-start(f32[1536,128]{1,0:T(8,128)S(1)} %get-tuple-element.14.in_s) | copy-start | bytes 2359300
  78.0 0.9 %copy-start.3 = (bf16[3072,128]{1,0:T(8,128)(2,1)}, bf16[3072,128]{1,0:T(8,128)(2,1)S(1)}, u32[]{:S(2)}) copy-start(bf16[3072,128]{1,0:T(8,128)(2,1)S(1)} %get-tuple-element.15.in_w) | copy-start | bytes 2359300

commit v4 on v3

--- a/solution.py
+++ b/solution.py
@@ -36,7 +36,9 @@
     main,
     alt,
     relay,
-    stage,
+    stage_m,
+    stage_f,
+    stage_s,
     edge,
     mine,
     theirs,
@@ -60,6 +62,7 @@
 ):
     olds = (old_m, old_f, old_s)
     outs = (out_m, out_f, out_s)
+    stages = (stage_m, stage_f, stage_s)
     old_cap = old_m.shape[0]
     half = mine.shape[0]
     size = half // CHUNKS
@@ -110,7 +113,6 @@
     for copy in offsets:
         copy.start()
     my_grads = pltpu.make_async_copy(grads.at[0, pl.ds(r * half, half)], mine, mine_sem)
-    my_grads.start()
 
     def load_own(k, rep):
         if rep == 0:
@@ -120,8 +122,8 @@
         return pltpu.make_async_copy(olds[k].at[pl.ds(JITTER, WINDOW)], main.at[k], in_sem.at[k])
 
     def load_stage(k):
-        rows = stage.shape[1]
-        return pltpu.make_async_copy(olds[k].at[pl.ds(old_cap - rows, rows)], stage.at[k], stage_sem.at[k])
+        rows = stage_m.shape[0]
+        return pltpu.make_async_copy(olds[k].at[pl.ds(old_cap - rows, rows)], stages[k], stage_sem.at[k])
 
     def die_copy(k, rep):
         first = 1024 if rep == 0 else 2560
@@ -230,18 +232,6 @@
             res.at[k, pl.ds(first, size)], outs[k].at[pl.ds(first, size)], res_sem.at[k, c]
         )
 
-    for rep in (0, 1):
-
-        @pl.when(even & (r == rep))
-        def _():
-            for k in range(3):
-                load_own(k, rep).start()
-
-    @pl.when(sends_head)
-    def _():
-        for k in range(3):
-            load_stage(k).start()
-
     barrier = pltpu.get_barrier_semaphore()
     pl.semaphore_signal(barrier, inc=1, device_id=other, device_id_type=MESH)
 
@@ -276,6 +266,11 @@
     @pl.when(relays_tail)
     def _():
         pl.semaphore_signal(barrier, inc=1, device_id=(r, lax.rem(tail_source, count)), device_id_type=MESH)
+
+    @pl.when(sends_head)
+    def _():
+        for k in range(3):
+            load_stage(k).start()
 
     targets = 1
     for cond, more in (
@@ -317,16 +312,24 @@
     for copy in offsets:
         copy.wait()
 
+    for rep in (0, 1):
+
+        @pl.when(even & (r == rep))
+        def _():
+            for k in range(3):
+                load_own(k, rep).start()
+
+    my_grads.start()
+
     @pl.when(sends_head)
     def _():
-        begin = within(old_off[o + 1] - old_off[o] - (old_cap - stage.shape[1]) - EDGE)
+        begin = within(old_off[o + 1] - old_off[o] - (old_cap - stage_m.shape[0]) - EDGE)
         for k in range(3):
             load_stage(k).wait()
-        for k in range(3):
 
             @pl.loop(0, EDGE // SUB)
             def _(j):
-                edge[k, pl.ds(pl.multiple_of(j * SUB, SUB), SUB), :] = stage[k, pl.ds(begin + j * SUB, SUB), :]
+                edge[k, pl.ds(pl.multiple_of(j * SUB, SUB), SUB), :] = stages[k][pl.ds(begin + j * SUB, SUB), :]
 
             @pl.when(x < 3)
             def _():
@@ -481,13 +484,17 @@
         wts_arrival(c).wait_recv()
 
 
-def finish(in_m, in_f, in_s, in_w, out_m, out_f, out_s, out_w, sem):
-    pairs = ((in_m, out_m), (in_f, out_f), (in_s, out_s), (in_w, out_w))
-    copies = [pltpu.make_async_copy(src, dst, sem.at[i]) for i, (src, dst) in enumerate(pairs)]
-    for copy in copies:
-        copy.start()
-    for copy in copies:
-        copy.wait()
+def finish(in_m, in_f, in_s, in_w, out_m, out_f, out_s, out_w, vm, vf, vs, vw, in_sem, out_sem):
+    ins, holds, outs = (in_m, in_f, in_s, in_w), (vm, vf, vs, vw), (out_m, out_f, out_s, out_w)
+    loads = [pltpu.make_async_copy(ins[i], holds[i], in_sem.at[i]) for i in range(4)]
+    stores = [pltpu.make_async_copy(holds[i], outs[i], out_sem.at[i]) for i in range(4)]
+    for load in loads:
+        load.start()
+    for load, store in zip(loads, stores):
+        load.wait()
+        store.start()
+    for store in stores:
+        store.wait()
 
 
 def local(old_master, old_first, old_second, grad_parts, old_offsets, new_offsets):
@@ -509,7 +516,9 @@
             pltpu.VMEM((3, WINDOW, lanes), jnp.float32),
             pltpu.VMEM((3, WINDOW, lanes), jnp.float32),
             pltpu.VMEM((2, 3, EDGE // 4, lanes), jnp.float32),
-            pltpu.VMEM((3, 3 * EDGE, lanes), jnp.float32),
+            pltpu.VMEM((3 * EDGE, lanes), jnp.float32),
+            pltpu.VMEM((3 * EDGE, lanes), jnp.float32),
+            pltpu.VMEM((3 * EDGE, lanes), jnp.float32),
             pltpu.VMEM((3, EDGE, lanes), jnp.float32),
             pltpu.VMEM((half, lanes), jnp.float32),
             pltpu.VMEM((half, lanes), jnp.float32),
@@ -532,16 +541,17 @@
             dma((CHUNKS,)),
         ],
         compiler_params=pltpu.CompilerParams(
-            collective_id=0, has_side_effects=True, vmem_limit_bytes=50 * 1024 * 1024
+            collective_id=0, has_side_effects=True, vmem_limit_bytes=60 * 1024 * 1024
         ),
         name="move_and_update",
     )(old_offsets, new_offsets, old_master, old_first, old_second, grad_parts)
     master, first, second, weights = pl.pallas_call(
         finish,
         out_shape=shapes,
-        in_specs=[pl.BlockSpec(memory_space=pltpu.VMEM)] * 4,
+        in_specs=[hbm] * 4,
         out_specs=(hbm,) * 4,
-        scratch_shapes=[dma((4,))],
+        scratch_shapes=[pltpu.VMEM(shape.shape, shape.dtype) for shape in shapes] + [dma((4,)), dma((4,))],
+        compiler_params=pltpu.CompilerParams(vmem_limit_bytes=60 * 1024 * 1024),
         name="finish",
     )(*results)
     return (master[None, None], first[None, None], second[None, None], weights)

time: 82.5 us -> 76.3 us (0.925)
  local copies, waits for them, and re-layouts: 4.87 us -> 0 us
  Pallas kernels: 76.8 us -> 75.6 us
    unnamed x12 -> x0, local copies, waits for them, and re-layouts: 4.87 us -> none
where the time goes in v4:
time: 76.3 us; the launch traced here: 76.2 us
  Pallas kernels  75.6 us (99%)
    pallas_call x1, Pallas kernels, local(): pl.pallas_call(kernel, out_shape=shapes, in_specs=[hbm] * 6, out_specs=(f...  72.7 us
    pallas_call x1, Pallas kernels, local(): pl.pallas_call(finish, out_shape=shapes, in_specs=[hbm] * 4, out_specs=(h...  2.86 us

profile of v4, /device:TPU:8, one launch (start us, length us, event | category | flops | bytes accessed | tf_op | source)
XLA Modules:
  0.0 76.2 jit_solution(17918332910355592988)
XLA Ops:
  0.6 72.7 %move_and_update.1 = (f32[1536,128]{1,0:T(8,128)}, f32[1536,128]{1,0:T(8,128)}, f32[1536,128]{1,0:T(8,128)}, bf16[3072,128]{1,0:T(8,128)(2,1)}) custom-call(s32[65]{0:T(128)} %old_off_in.1, s32[129]{0:T(256)} %new_off_in.1, f32[5120,128]{1,0:T(8,128)} %old_m.1, f32[5120,128]{1,0:T(8,128)} %old_f.1, f32[5120,128]{1,0:T(8,128)} %old_s.1, f32[1,3072,128]{2,1,0:T(8,128)} %grads.1), custom_call_target="tpu_custom_call" | custom-call | tf_op jit(solution)/shard_map/move_and_update/pallas_call | solution.py:508
  73.4 2.9 %finish.1 = (f32[1536,128]{1,0:T(8,128)}, f32[1536,128]{1,0:T(8,128)}, f32[1536,128]{1,0:T(8,128)}, bf16[3072,128]{1,0:T(8,128)(2,1)}) custom-call(f32[1536,128]{1,0:T(8,128)} %get-tuple-element.12.in_m, f32[1536,128]{1,0:T(8,128)} %get-tuple-element.13.in_f, f32[1536,128]{1,0:T(8,128)} %get-tuple-element.14.in_s, bf16[3072,128]{1,0:T(8,128)(2,1)} %get-tuple-element.15.in_w), custom_call_target="tpu_custom_call" | custom-call | tf_op jit(solution)/shard_map/finish/pallas_call | solution.py:548

commit v5 on v4

--- a/solution.py
+++ b/solution.py
@@ -14,6 +14,7 @@
 WINDOW = 3584
 CHUNKS = 8
 SUB = 64
+EARLY = 3
 
 
 def within(start):
@@ -77,8 +78,8 @@
 
     x = o % 4
 
-    up_rep = jnp.where(o % 16 == 15, 1 - r, r)
-    down_rep = jnp.where(o % 16 == 0, 1 - r, r)
+    up_rep = r
+    down_rep = r
     sends_head = even & (up_rep == 0) & (o < owners - 1)
     gets_head = even & (r == 0) & (o > 0)
     sends_tail = even & (o > 0)
@@ -98,10 +99,10 @@
     tail_wraps = sends_tail & (x == 0)
     tail_unwraps = gets_tail & (x == 3)
     head_source = s - 1 + 2 * (3 - x) - turn_up
-    head_rep = jnp.where(z_lo == 3, 1 - r, r)
+    head_rep = r
     relays_head = odd & (head_rep == 0) & (head_source >= 0)
     tail_source = s - 1 - 2 * x + turn_down
-    tail_rep = jnp.where(z_lo == 0, 1 - r, r)
+    tail_rep = r
     relays_tail = odd & (tail_source < count)
     head_relays = s + jnp.where(z_lo == 0, 24, -8) + 1
     tail_relays = s + jnp.where(z_lo == 3, -24, 8) - 6
@@ -232,6 +233,11 @@
             res.at[k, pl.ds(first, size)], outs[k].at[pl.ds(first, size)], res_sem.at[k, c]
         )
 
+    @pl.when(sends_head)
+    def _():
+        for k in range(3):
+            load_stage(k).start()
+
     barrier = pltpu.get_barrier_semaphore()
     pl.semaphore_signal(barrier, inc=1, device_id=other, device_id_type=MESH)
 
@@ -266,11 +272,6 @@
     @pl.when(relays_tail)
     def _():
         pl.semaphore_signal(barrier, inc=1, device_id=(r, lax.rem(tail_source, count)), device_id_type=MESH)
-
-    @pl.when(sends_head)
-    def _():
-        for k in range(3):
-            load_stage(k).start()
 
     targets = 1
     for cond, more in (
@@ -298,28 +299,14 @@
                 for k in range(3):
                     tail_relay_in(k, rep, part).start()
 
-    @pl.loop(0, CHUNKS)
+    early = jnp.where(odd, EARLY, CHUNKS)
+
+    @pl.loop(0, early)
     def _(c):
         grad_copy(c).start()
 
-    for rep in (0, 1):
-
-        @pl.when(even & (r == rep))
-        def _():
-            for k in range(3):
-                die_copy(k, rep).start()
-
     for copy in offsets:
         copy.wait()
-
-    for rep in (0, 1):
-
-        @pl.when(even & (r == rep))
-        def _():
-            for k in range(3):
-                load_own(k, rep).start()
-
-    my_grads.start()
 
     @pl.when(sends_head)
     def _():
@@ -339,6 +326,22 @@
             def _():
                 for part in range(4):
                     head_relay_in(k, part).start()
+
+    for rep in (0, 1):
+
+        @pl.when(even & (r == rep))
+        def _():
+            for k in range(3):
+                die_copy(k, rep).start()
+
+    for rep in (0, 1):
+
+        @pl.when(even & (r == rep))
+        def _():
+            for k in range(3):
+                load_own(k, rep).start()
+
+    my_grads.start()
 
     for rep in (0, 1):
         for part in range(4):
@@ -356,6 +359,10 @@
             for k in range(3):
                 head_relay_in(k, part).wait_recv()
                 head_relay_out(k, part).start()
+
+    @pl.loop(early, CHUNKS)
+    def _(c):
+        grad_copy(c).start()
 
     for rep in (0, 1):
 

time: 76.3 us -> 72 us (0.944)
  the two profiles are of different devices: /device:TPU:8 before, /device:TPU:29 now
where the time goes in v5:
time: 72 us; the launch traced here: 71.8 us
  Pallas kernels  71.2 us (99%)
    pallas_call x1, Pallas kernels, local(): pl.pallas_call(kernel, out_shape=shapes, in_specs=[hbm] * 6, out_specs=(f...  68.3 us
    pallas_call x1, Pallas kernels, local(): pl.pallas_call(finish, out_shape=shapes, in_specs=[hbm] * 4, out_specs=(h...  2.86 us

profile of v5, /device:TPU:29, one launch (start us, length us, event | category | flops | bytes accessed | tf_op | source)
XLA Modules:
  0.0 71.8 jit_solution(5375883258838621576)
XLA Ops:
  0.6 68.3 %move_and_update.1 = (f32[1536,128]{1,0:T(8,128)}, f32[1536,128]{1,0:T(8,128)}, f32[1536,128]{1,0:T(8,128)}, bf16[3072,128]{1,0:T(8,128)(2,1)}) custom-call(s32[65]{0:T(128)} %old_off_in.1, s32[129]{0:T(256)} %new_off_in.1, f32[5120,128]{1,0:T(8,128)} %old_m.1, f32[5120,128]{1,0:T(8,128)} %old_f.1, f32[5120,128]{1,0:T(8,128)} %old_s.1, f32[1,3072,128]{2,1,0:T(8,128)} %grads.1), custom_call_target="tpu_custom_call" | custom-call | tf_op jit(solution)/shard_map/move_and_update/pallas_call | solution.py:515
  69.0 2.9 %finish.1 = (f32[1536,128]{1,0:T(8,128)}, f32[1536,128]{1,0:T(8,128)}, f32[1536,128]{1,0:T(8,128)}, bf16[3072,128]{1,0:T(8,128)(2,1)}) custom-call(f32[1536,128]{1,0:T(8,128)} %get-tuple-element.12.in_m, f32[1536,128]{1,0:T(8,128)} %get-tuple-element.13.in_f, f32[1536,128]{1,0:T(8,128)} %get-tuple-element.14.in_s, bf16[3072,128]{1,0:T(8,128)(2,1)} %get-tuple-element.15.in_w), custom_call_target="tpu_custom_call" | custom-call | tf_op jit(solution)/shard_map/finish/pallas_call | solution.py:555

commit v6 on v5

--- a/solution.py
+++ b/solution.py
@@ -11,10 +11,11 @@
 MESH = pl.DeviceIdType.MESH
 JITTER = 512
 EDGE = 2 * JITTER
+PACK = 1024
 WINDOW = 3584
 CHUNKS = 8
 SUB = 64
-EARLY = 3
+EARLY = 4
 
 
 def within(start):
@@ -43,6 +44,10 @@
     edge,
     mine,
     theirs,
+    near_grads,
+    far_grads,
+    pack,
+    packed,
     res,
     wts,
     off_sem,
@@ -54,6 +59,8 @@
     tail_sem,
     head_relay_sem,
     tail_relay_sem,
+    pack_sem,
+    pass_sem,
     grad_send,
     grad_recv,
     wts_send,
@@ -186,16 +193,43 @@
         to = (tail_rep, lax.rem(tail_source + count - 1, count))
         return send(relay.at[1, k, pl.ds(0, rows)], alt.at[k, pl.ds(first + part * rows, rows)], sems, to)
 
-    def grad_copy(c):
-        first = pl.multiple_of(c * size, 16)
-        return pltpu.make_async_remote_copy(
-            grads.at[0, pl.ds(pl.multiple_of((1 - r) * half + first, 16), size)],
-            theirs.at[pl.ds(first, size)],
-            grad_send.at[c],
-            grad_recv.at[c],
-            device_id=other,
-            device_id_type=MESH,
-        )
+    piece = PACK // CHUNKS
+
+    def grad_copy(c, rep):
+        if rep == 1:
+            rows = pl.ds(pl.multiple_of(c * size, 16), size)
+            src, dst = grads.at[0, rows], theirs.at[rows]
+        else:
+            src = pack.at[pl.ds(pl.multiple_of(c * piece, 16), piece)]
+            dst = packed.at[pl.ds(pl.multiple_of(core * PACK + c * piece, 16), piece)]
+        return send(src, dst, (grad_send.at[c], grad_recv.at[c]), other)
+
+    def pass_copy(c):
+        rows = packed.at[pl.ds(pl.multiple_of(core * PACK + c * piece, 16), piece)]
+        return send(rows, rows, (pass_sem.at[0, c], pass_sem.at[1, c]), die_to)
+
+    def near_copy(at):
+        if at == 0:
+            return pltpu.make_async_copy(grads.at[0, pl.ds(half, PACK)], near_grads, pack_sem.at[0])
+        rows = half - PACK
+        sems = (pack_sem.at[1], pack_sem.at[2])
+        return send(grads.at[0, pl.ds(half + PACK, rows)], near_grads.at[pl.ds(0, rows)], sems, die_to)
+
+    def far_copy(at):
+        if at == 1:
+            rows = far_grads.at[pl.ds(half - PACK, half)]
+            return pltpu.make_async_copy(grads.at[0, pl.ds(half, half)], rows, pack_sem.at[0])
+        sems = (pack_sem.at[1], pack_sem.at[2])
+        return send(grads.at[0, pl.ds(half, PACK)], far_grads.at[pl.ds(half, PACK)], sems, die_to)
+
+    def start_grads(first, last):
+        for rep in (0, 1):
+
+            @pl.when(r == rep)
+            def _():
+                @pl.loop(first, last)
+                def _(c):
+                    grad_copy(c, rep).start()
 
     def wts_copy(c):
         first = pl.multiple_of(c * size, 16)
@@ -238,12 +272,18 @@
         for k in range(3):
             load_stage(k).start()
 
+    @pl.when((r == 0) & even)
+    def _():
+        near_copy(0).start()
+
+    @pl.when((r == 0) & odd)
+    def _():
+        far_copy(1).start()
+
     barrier = pltpu.get_barrier_semaphore()
     pl.semaphore_signal(barrier, inc=1, device_id=other, device_id_type=MESH)
 
-    @pl.when(odd)
-    def _():
-        pl.semaphore_signal(barrier, inc=1, device_id=die_to, device_id_type=MESH)
+    pl.semaphore_signal(barrier, inc=1, device_id=die_to, device_id_type=MESH)
 
     @pl.when(gets_head & (x > 0))
     def _():
@@ -273,9 +313,8 @@
     def _():
         pl.semaphore_signal(barrier, inc=1, device_id=(r, lax.rem(tail_source, count)), device_id_type=MESH)
 
-    targets = 1
+    targets = 2
     for cond, more in (
-        (even, 1),
         (sends_head, 1),
         (head_wraps, 3),
         (sends_tail, 1),
@@ -286,12 +325,23 @@
         targets = targets + more * cond.astype(jnp.int32)
     pl.semaphore_wait(barrier, targets)
 
-    for rep in (0, 1):
-
-        @pl.when(sends_tail & (down_rep == rep) & (x > 0))
-        def _():
-            for k in range(3):
-                tail_copy(k, rep).start()
+    early = jnp.where(odd, EARLY, CHUNKS)
+
+    @pl.when(r == 1)
+    def _():
+        @pl.loop(0, early)
+        def _(c):
+            grad_copy(c, 1).start()
+
+    @pl.when((r == 0) & even)
+    def _():
+        near_copy(1).start()
+
+    @pl.when((r == 0) & odd)
+    def _():
+        far_copy(0).start()
+
+    for rep in (0, 1):
 
         @pl.when(tail_wraps & (down_rep == rep))
         def _():
@@ -299,14 +349,37 @@
                 for k in range(3):
                     tail_relay_in(k, rep, part).start()
 
-    early = jnp.where(odd, EARLY, CHUNKS)
-
-    @pl.loop(0, early)
-    def _(c):
-        grad_copy(c).start()
-
     for copy in offsets:
         copy.wait()
+
+    pair = s - core
+    first_rows = jnp.clip(new_off[pair + 1] - new_off[pair] - half, 0, half)
+
+    @pl.when((r == 0) & even)
+    def _():
+        near_copy(0).wait()
+        far_copy(0).wait_recv()
+
+    @pl.when((r == 0) & odd)
+    def _():
+        far_copy(1).wait()
+        near_copy(1).wait_recv()
+
+    @pl.when(r == 0)
+    def _():
+        @pl.loop(0, PACK // SUB)
+        def _(j):
+            at = j * SUB
+            rows = pl.ds(pl.multiple_of(at, SUB), SUB)
+            row = core * PACK + at + lax.broadcasted_iota(jnp.int32, (SUB, 128), 0)
+            far = far_grads[pl.ds(half - first_rows + at, SUB), :]
+            pack[rows, :] = jnp.where(row < first_rows, near_grads[rows, :], far)
+
+    @pl.when(r == 0)
+    def _():
+        @pl.loop(0, CHUNKS)
+        def _(c):
+            grad_copy(c, 0).start()
 
     @pl.when(sends_head)
     def _():
@@ -329,6 +402,13 @@
 
     for rep in (0, 1):
 
+        @pl.when(sends_tail & (down_rep == rep) & (x > 0))
+        def _():
+            for k in range(3):
+                tail_copy(k, rep).start()
+
+    for rep in (0, 1):
+
         @pl.when(even & (r == rep))
         def _():
             for k in range(3):
@@ -342,6 +422,14 @@
                 load_own(k, rep).start()
 
     my_grads.start()
+
+    for part in range(4):
+
+        @pl.when(relays_head & (x == part))
+        def _():
+            for k in range(3):
+                head_relay_in(k, part).wait_recv()
+                head_relay_out(k, part).start()
 
     for rep in (0, 1):
         for part in range(4):
@@ -352,17 +440,24 @@
                     tail_relay_in(k, rep, part).wait_recv()
                     tail_relay_out(k, rep, part).start()
 
-    for part in range(4):
-
-        @pl.when(relays_head & (x == part))
-        def _():
-            for k in range(3):
-                head_relay_in(k, part).wait_recv()
-                head_relay_out(k, part).start()
-
-    @pl.loop(early, CHUNKS)
-    def _(c):
-        grad_copy(c).start()
+    @pl.when(r == 1)
+    def _():
+        @pl.loop(early, CHUNKS)
+        def _(c):
+            grad_copy(c, 1).start()
+
+    passes = jnp.where(even, CHUNKS, (half - PACK) // piece)
+    arrivals = jnp.where(odd, CHUNKS, (half - PACK) // piece)
+
+    @pl.when(r == 1)
+    def _():
+        @pl.loop(0, CHUNKS)
+        def _(c):
+            grad_copy(c, 0).wait_recv()
+
+            @pl.when(c < passes)
+            def _():
+                pass_copy(c).start()
 
     for rep in (0, 1):
 
@@ -408,10 +503,7 @@
     flat = new_off[s] + r * half
     stop = new_off[s + 1]
 
-    @pl.loop(0, CHUNKS)
-    def _(c):
-        grad_copy(c).wait_recv()
-
+    def update(c, their_rows):
         @pl.loop(0, size // SUB)
         def _(j):
             at = c * size + j * SUB
@@ -423,7 +515,7 @@
                 jnp.where(near, main[k, pl.ds(start + at, SUB), :], alt[k, pl.ds(edge_start + at, SUB), :])
                 for k in range(3)
             ]
-            total = mine[rows, :] + theirs[rows, :]
+            total = mine[rows, :] + their_rows(at)
             first_n = 0.9 * first + 0.1 * total
             second_n = 0.95 * second + 0.05 * total * total
             first_hat = first_n / (1.0 - 0.9**STEP)
@@ -440,6 +532,24 @@
         for k in range(3):
             res_copy(k, c).start()
 
+    @pl.when(r == 0)
+    def _():
+        @pl.loop(0, CHUNKS)
+        def _(c):
+            grad_copy(c, 1).wait_recv()
+            update(c, lambda at: theirs[pl.ds(pl.multiple_of(at, SUB), SUB), :])
+
+    @pl.when(r == 1)
+    def _():
+        @pl.loop(0, arrivals)
+        def _(c):
+            there = packed.at[pl.ds(pl.multiple_of((1 - core) * PACK + c * piece, 16), piece)]
+            send(there, there, (pass_sem.at[0, c], pass_sem.at[1, c]), die_to).wait_recv()
+
+        @pl.loop(0, CHUNKS)
+        def _(c):
+            update(c, lambda at: packed[pl.ds(core * first_rows + at, SUB), :])
+
     for rep in (0, 1):
 
         @pl.when(even & (r == rep))
@@ -481,9 +591,30 @@
             for k in range(3):
                 tail_relay_out(k, rep, 0).wait_send()
 
+    @pl.when((r == 0) & even)
+    def _():
+        near_copy(1).wait_send()
+
+    @pl.when((r == 0) & odd)
+    def _():
+        far_copy(0).wait_send()
+
+    @pl.when(r == 1)
+    def _():
+        @pl.loop(0, passes)
+        def _(c):
+            pass_copy(c).wait_send()
+
+    for rep in (0, 1):
+
+        @pl.when(r == rep)
+        def _():
+            @pl.loop(0, CHUNKS)
+            def _(c):
+                grad_copy(c, rep).wait_send()
+
     @pl.loop(0, CHUNKS)
     def _(c):
-        grad_copy(c).wait_send()
         for k in range(3):
             res_copy(k, c).wait()
         own_copy(c).wait()
@@ -529,6 +660,10 @@
             pltpu.VMEM((3, EDGE, lanes), jnp.float32),
             pltpu.VMEM((half, lanes), jnp.float32),
             pltpu.VMEM((half, lanes), jnp.float32),
+            pltpu.VMEM((PACK, lanes), jnp.float32),
+            pltpu.VMEM((half + PACK, lanes), jnp.float32),
+            pltpu.VMEM((PACK, lanes), jnp.float32),
+            pltpu.VMEM((2 * half, lanes), jnp.float32),
             pltpu.VMEM((3, half, lanes), jnp.float32),
             pltpu.VMEM((half, lanes), jnp.bfloat16),
             dma((2,)),
@@ -540,6 +675,8 @@
             dma((2, 4, 3)),
             dma((2, 3)),
             dma((2, 3)),
+            dma((3,)),
+            dma((2, CHUNKS)),
             dma((CHUNKS,)),
             dma((CHUNKS,)),
             dma((CHUNKS,)),

time: 72 us -> 70.2 us (0.975)
  the two profiles are of different devices: /device:TPU:29 before, /device:TPU:41 now
where the time goes in v6:
time: 70.2 us; the launch traced here: 70.1 us
  Pallas kernels  69.5 us (99%)
    pallas_call x1, Pallas kernels, local(): pl.pallas_call(kernel, out_shape=shapes, in_specs=[hbm] * 6, out_specs=(f...  66.6 us
    pallas_call x1, Pallas kernels, local(): pl.pallas_call(finish, out_shape=shapes, in_specs=[hbm] * 4, out_specs=(h...  2.86 us

profile of v6, /device:TPU:41, one launch (start us, length us, event | category | flops | bytes accessed | tf_op | source)
XLA Modules:
  0.0 70.1 jit_solution(5566079848486275648)
XLA Ops:
  0.6 66.6 %move_and_update.1 = (f32[1536,128]{1,0:T(8,128)}, f32[1536,128]{1,0:T(8,128)}, f32[1536,128]{1,0:T(8,128)}, bf16[3072,128]{1,0:T(8,128)(2,1)}) custom-call(s32[65]{0:T(128)} %old_off_in.1, s32[129]{0:T(256)} %new_off_in.1, f32[5120,128]{1,0:T(8,128)} %old_m.1, f32[5120,128]{1,0:T(8,128)} %old_f.1, f32[5120,128]{1,0:T(8,128)} %old_s.1, f32[1,3072,128]{2,1,0:T(8,128)} %grads.1), custom_call_target="tpu_custom_call" | custom-call | tf_op jit(solution)/shard_map/move_and_update/pallas_call | solution.py:646
  67.3 2.9 %finish.1 = (f32[1536,128]{1,0:T(8,128)}, f32[1536,128]{1,0:T(8,128)}, f32[1536,128]{1,0:T(8,128)}, bf16[3072,128]{1,0:T(8,128)(2,1)}) custom-call(f32[1536,128]{1,0:T(8,128)} %get-tuple-element.12.in_m, f32[1536,128]{1,0:T(8,128)} %get-tuple-element.13.in_f, f32[1536,128]{1,0:T(8,128)} %get-tuple-element.14.in_s, bf16[3072,128]{1,0:T(8,128)(2,1)} %get-tuple-element.15.in_w), custom_call_target="tpu_custom_call" | custom-call | tf_op jit(solution)/shard_map/finish/pallas_call | solution.py:692

commit v7 on v6

--- a/solution.py
+++ b/solution.py
@@ -15,7 +15,7 @@
 WINDOW = 3584
 CHUNKS = 8
 SUB = 64
-EARLY = 4
+EARLY = 5
 
 
 def within(start):
@@ -33,6 +33,7 @@
     out_f,
     out_s,
     out_w,
+    out_q,
     old_off,
     new_off,
     main,
@@ -44,10 +45,12 @@
     edge,
     mine,
     theirs,
-    near_grads,
-    far_grads,
+    near_rows,
+    far_rows,
     pack,
     packed,
+    short_pack,
+    short_packed,
     res,
     wts,
     off_sem,
@@ -67,6 +70,7 @@
     wts_recv,
     res_sem,
     own_sem,
+    short_sem,
 ):
     olds = (old_m, old_f, old_s)
     outs = (out_m, out_f, out_s)
@@ -208,19 +212,43 @@
         rows = packed.at[pl.ds(pl.multiple_of(core * PACK + c * piece, 16), piece)]
         return send(rows, rows, (pass_sem.at[0, c], pass_sem.at[1, c]), die_to)
 
-    def near_copy(at):
+    def grad_rows(first, rows):
+        return grads.at[0, pl.ds(half + first, rows)]
+
+    def master_rows(first, rows):
+        return res.at[0, pl.ds(first, rows)]
+
+    def near_copy(at, source):
         if at == 0:
-            return pltpu.make_async_copy(grads.at[0, pl.ds(half, PACK)], near_grads, pack_sem.at[0])
+            return pltpu.make_async_copy(source(0, PACK), near_rows, pack_sem.at[0])
         rows = half - PACK
-        sems = (pack_sem.at[1], pack_sem.at[2])
-        return send(grads.at[0, pl.ds(half + PACK, rows)], near_grads.at[pl.ds(0, rows)], sems, die_to)
-
-    def far_copy(at):
+        return send(source(PACK, rows), near_rows.at[pl.ds(0, rows)], (pack_sem.at[1], pack_sem.at[2]), die_to)
+
+    def far_copy(at, source):
         if at == 1:
-            rows = far_grads.at[pl.ds(half - PACK, half)]
-            return pltpu.make_async_copy(grads.at[0, pl.ds(half, half)], rows, pack_sem.at[0])
-        sems = (pack_sem.at[1], pack_sem.at[2])
-        return send(grads.at[0, pl.ds(half, PACK)], far_grads.at[pl.ds(half, PACK)], sems, die_to)
+            return pltpu.make_async_copy(source(0, half), far_rows.at[pl.ds(half - PACK, half)], pack_sem.at[0])
+        return send(source(0, PACK), far_rows.at[pl.ds(half, PACK)], (pack_sem.at[1], pack_sem.at[2]), die_to)
+
+    def pack_rows(at):
+        row = core * PACK + at + lax.broadcasted_iota(jnp.int32, (SUB, 128), 0)
+        far = far_rows[pl.ds(half - first_rows + at, SUB), :]
+        return jnp.where(row < first_rows, near_rows[pl.ds(pl.multiple_of(at, SUB), SUB), :], far)
+
+    def short_copy(c):
+        src = short_pack.at[pl.ds(pl.multiple_of(c * piece, 16), piece)]
+        dst = short_packed.at[pl.ds(pl.multiple_of(core * PACK + c * piece, 16), piece)]
+        return send(src, dst, (wts_send.at[c], wts_recv.at[c]), other)
+
+    def short_place(c, at):
+        return pl.ds(pl.multiple_of(at * PACK + c * piece, 16), piece)
+
+    def short_pass(c, at):
+        rows = short_place(c, at)
+        return send(short_packed.at[rows], out_q.at[rows], (pass_sem.at[0, c], pass_sem.at[1, c]), die_to)
+
+    def short_keep(c):
+        rows = short_place(c, core)
+        return pltpu.make_async_copy(short_packed.at[rows], out_q.at[rows], short_sem.at[c])
 
     def start_grads(first, last):
         for rep in (0, 1):
@@ -274,11 +302,11 @@
 
     @pl.when((r == 0) & even)
     def _():
-        near_copy(0).start()
+        near_copy(0, grad_rows).start()
 
     @pl.when((r == 0) & odd)
     def _():
-        far_copy(1).start()
+        far_copy(1, grad_rows).start()
 
     barrier = pltpu.get_barrier_semaphore()
     pl.semaphore_signal(barrier, inc=1, device_id=other, device_id_type=MESH)
@@ -335,11 +363,11 @@
 
     @pl.when((r == 0) & even)
     def _():
-        near_copy(1).start()
+        near_copy(1, grad_rows).start()
 
     @pl.when((r == 0) & odd)
     def _():
-        far_copy(0).start()
+        far_copy(0, grad_rows).start()
 
     for rep in (0, 1):
 
@@ -357,23 +385,19 @@
 
     @pl.when((r == 0) & even)
     def _():
-        near_copy(0).wait()
-        far_copy(0).wait_recv()
+        near_copy(0, grad_rows).wait()
+        far_copy(0, grad_rows).wait_recv()
 
     @pl.when((r == 0) & odd)
     def _():
-        far_copy(1).wait()
-        near_copy(1).wait_recv()
+        far_copy(1, grad_rows).wait()
+        near_copy(1, grad_rows).wait_recv()
 
     @pl.when(r == 0)
     def _():
         @pl.loop(0, PACK // SUB)
         def _(j):
-            at = j * SUB
-            rows = pl.ds(pl.multiple_of(at, SUB), SUB)
-            row = core * PACK + at + lax.broadcasted_iota(jnp.int32, (SUB, 128), 0)
-            far = far_grads[pl.ds(half - first_rows + at, SUB), :]
-            pack[rows, :] = jnp.where(row < first_rows, near_grads[rows, :], far)
+            pack[pl.ds(pl.multiple_of(j * SUB, SUB), SUB), :] = pack_rows(j * SUB)
 
     @pl.when(r == 0)
     def _():
@@ -527,7 +551,6 @@
             res[2, rows, :] = jnp.where(keep, second_n, 0.0)
             wts[rows, :] = master_n.astype(jnp.bfloat16)
 
-        wts_copy(c).start()
         own_copy(c).start()
         for k in range(3):
             res_copy(k, c).start()
@@ -538,6 +561,17 @@
         def _(c):
             grad_copy(c, 1).wait_recv()
             update(c, lambda at: theirs[pl.ds(pl.multiple_of(at, SUB), SUB), :])
+            wts_copy(c).start()
+
+        @pl.loop(0, CHUNKS)
+        def _(c):
+            short_copy(c).wait_recv()
+            short_keep(c).start()
+
+            @pl.when(c < passes)
+            def _():
+                short_pass(c, core).start()
+
 
     @pl.when(r == 1)
     def _():
@@ -549,6 +583,36 @@
         @pl.loop(0, CHUNKS)
         def _(c):
             update(c, lambda at: packed[pl.ds(core * first_rows + at, SUB), :])
+
+            @pl.when((c == (PACK - 1) // size) & even)
+            def _():
+                near_copy(0, master_rows).start()
+
+            @pl.when((c == (PACK - 1) // size) & odd)
+            def _():
+                far_copy(0, master_rows).start()
+
+        @pl.when(even)
+        def _():
+            near_copy(1, master_rows).start()
+            near_copy(0, master_rows).wait()
+            far_copy(0, master_rows).wait_recv()
+
+        @pl.when(odd)
+        def _():
+            far_copy(1, master_rows).start()
+            far_copy(1, master_rows).wait()
+            near_copy(1, master_rows).wait_recv()
+
+        @pl.loop(0, CHUNKS)
+        def _(c):
+            @pl.loop(0, piece // SUB)
+            def _(j):
+                at = c * piece + j * SUB
+                short_pack[pl.ds(pl.multiple_of(at, SUB), SUB), :] = pack_rows(at).astype(jnp.bfloat16)
+
+            short_copy(c).start()
+
 
     for rep in (0, 1):
 
@@ -591,19 +655,13 @@
             for k in range(3):
                 tail_relay_out(k, rep, 0).wait_send()
 
-    @pl.when((r == 0) & even)
-    def _():
-        near_copy(1).wait_send()
-
-    @pl.when((r == 0) & odd)
-    def _():
-        far_copy(0).wait_send()
-
-    @pl.when(r == 1)
-    def _():
-        @pl.loop(0, passes)
-        def _(c):
-            pass_copy(c).wait_send()
+    @pl.when(even)
+    def _():
+        near_copy(1, grad_rows).wait_send()
+
+    @pl.when(odd)
+    def _():
+        far_copy(0, grad_rows).wait_send()
 
     for rep in (0, 1):
 
@@ -612,27 +670,95 @@
             @pl.loop(0, CHUNKS)
             def _(c):
                 grad_copy(c, rep).wait_send()
-
-    @pl.loop(0, CHUNKS)
-    def _(c):
-        for k in range(3):
-            res_copy(k, c).wait()
-        own_copy(c).wait()
-        wts_copy(c).wait_send()
-        wts_arrival(c).wait_recv()
-
-
-def finish(in_m, in_f, in_s, in_w, out_m, out_f, out_s, out_w, vm, vf, vs, vw, in_sem, out_sem):
-    ins, holds, outs = (in_m, in_f, in_s, in_w), (vm, vf, vs, vw), (out_m, out_f, out_s, out_w)
-    loads = [pltpu.make_async_copy(ins[i], holds[i], in_sem.at[i]) for i in range(4)]
-    stores = [pltpu.make_async_copy(holds[i], outs[i], out_sem.at[i]) for i in range(4)]
+                own_copy(c).wait()
+                for k in range(3):
+                    res_copy(k, c).wait()
+
+    @pl.when(r == 0)
+    def _():
+        @pl.loop(0, CHUNKS)
+        def _(c):
+            wts_copy(c).wait_send()
+            short_keep(c).wait()
+
+        @pl.loop(0, passes)
+        def _(c):
+            short_pass(c, core).wait_send()
+
+        @pl.loop(0, arrivals)
+        def _(c):
+            short_pass(c, 1 - core).wait_recv()
+
+    @pl.when(r == 1)
+    def _():
+        @pl.loop(0, passes)
+        def _(c):
+            pass_copy(c).wait_send()
+
+        @pl.loop(0, CHUNKS)
+        def _(c):
+            short_copy(c).wait_send()
+            wts_arrival(c).wait_recv()
+
+
+def finish(
+    off_in, in_m, in_f, in_s, in_w, in_q, out_m, out_f, out_s, out_w, off, vm, vf, vs, vw, vq, wide, in_sem, out_sem
+):
+    r = lax.axis_index("rep")
+    s = lax.axis_index("shard")
+    core = s % 2
+    half = vm.shape[0]
+    top, low = pl.ds(0, half), pl.ds(half, half)
+    load_off = pltpu.make_async_copy(off_in, off, in_sem.at[0])
+    load_q = pltpu.make_async_copy(in_q, vq, in_sem.at[1])
+    pairs = [(in_m, vm, out_m), (in_f, vf, out_f), (in_s, vs, out_s), (in_w.at[top], vw.at[top], out_w.at[top])]
+    loads = [pltpu.make_async_copy(src, hold, in_sem.at[2 + i]) for i, (src, hold, _) in enumerate(pairs)]
+    stores = [pltpu.make_async_copy(hold, dst, out_sem.at[i]) for i, (_, hold, dst) in enumerate(pairs)]
+    load_low = pltpu.make_async_copy(in_w.at[low], vw.at[low], in_sem.at[1])
+    store_low = pltpu.make_async_copy(vw.at[low], out_w.at[low], out_sem.at[4])
+    load_off.start()
+
+    @pl.when(r == 0)
+    def _():
+        load_q.start()
+
+    @pl.when(r == 1)
+    def _():
+        load_low.start()
+
     for load in loads:
         load.start()
+    load_off.wait()
+
+    @pl.when(r == 0)
+    def _():
+        pair = s - core
+        first_rows = jnp.clip(off[pair + 1] - off[pair] - half, 0, half)
+        live = off[s + 1] - off[s] - half
+        load_q.wait()
+
+        @pl.loop(0, vq.shape[0] // SUB)
+        def _(j):
+            rows = pl.ds(pl.multiple_of(j * SUB, SUB), SUB)
+            wide[rows, :] = vq[rows, :].astype(jnp.float32)
+
+        @pl.loop(0, half // SUB)
+        def _(j):
+            row = j * SUB + lax.broadcasted_iota(jnp.int32, (SUB, 128), 0)
+            mine = jnp.where(row < live, wide[pl.ds(core * first_rows + j * SUB, SUB), :], 0.0)
+            vw[pl.ds(pl.multiple_of(half + j * SUB, SUB), SUB), :] = mine.astype(jnp.bfloat16)
+
+    @pl.when(r == 1)
+    def _():
+        load_low.wait()
+
+    store_low.start()
     for load, store in zip(loads, stores):
         load.wait()
         store.start()
     for store in stores:
         store.wait()
+    store_low.wait()
 
 
 def local(old_master, old_first, old_second, grad_parts, old_offsets, new_offsets):
@@ -643,11 +769,12 @@
     state = jax.ShapeDtypeStruct((half, lanes), jnp.float32)
     dma = pltpu.SemaphoreType.DMA
     shapes = (state, state, state, jax.ShapeDtypeStruct((new_cap, lanes), jnp.bfloat16))
+    short = jax.ShapeDtypeStruct((2 * PACK, lanes), jnp.bfloat16)
     results = pl.pallas_call(
         kernel,
-        out_shape=shapes,
+        out_shape=shapes + (short,),
         in_specs=[hbm] * 6,
-        out_specs=(free, free, free, free),
+        out_specs=(free,) * 5,
         scratch_shapes=[
             pltpu.SMEM(old_offsets.shape, jnp.int32),
             pltpu.SMEM(new_offsets.shape, jnp.int32),
@@ -664,6 +791,8 @@
             pltpu.VMEM((half + PACK, lanes), jnp.float32),
             pltpu.VMEM((PACK, lanes), jnp.float32),
             pltpu.VMEM((2 * half, lanes), jnp.float32),
+            pltpu.VMEM((PACK, lanes), jnp.bfloat16),
+            pltpu.VMEM((2 * PACK, lanes), jnp.bfloat16),
             pltpu.VMEM((3, half, lanes), jnp.float32),
             pltpu.VMEM((half, lanes), jnp.bfloat16),
             dma((2,)),
@@ -683,6 +812,7 @@
             dma((CHUNKS,)),
             dma((3, CHUNKS)),
             dma((CHUNKS,)),
+            dma((CHUNKS,)),
         ],
         compiler_params=pltpu.CompilerParams(
             collective_id=0, has_side_effects=True, vmem_limit_bytes=60 * 1024 * 1024
@@ -692,12 +822,14 @@
     master, first, second, weights = pl.pallas_call(
         finish,
         out_shape=shapes,
-        in_specs=[hbm] * 4,
+        in_specs=[hbm] * 6,
         out_specs=(hbm,) * 4,
-        scratch_shapes=[pltpu.VMEM(shape.shape, shape.dtype) for shape in shapes] + [dma((4,)), dma((4,))],
+        scratch_shapes=[pltpu.SMEM(new_offsets.shape, jnp.int32)]
+        + [pltpu.VMEM(shape.shape, shape.dtype) for shape in shapes + (short,)]
+        + [pltpu.VMEM((new_cap, lanes), jnp.float32), dma((6,)), dma((5,))],
         compiler_params=pltpu.CompilerParams(vmem_limit_bytes=60 * 1024 * 1024),
         name="finish",
-    )(*results)
+    )(new_offsets, *results)
     return (master[None, None], first[None, None], second[None, None], weights)
 
 

time: 70.2 us -> 67.7 us (0.964)
  the two profiles are of different devices: /device:TPU:41 before, /device:TPU:55 now
where the time goes in v7:
time: 67.7 us; the launch traced here: 67.6 us
  Pallas kernels  67 us (99%)
    pallas_call x1, Pallas kernels, local(): pl.pallas_call(kernel, out_shape=shapes + (short,), in_specs=[hbm] * 6, o...  63.8 us
    pallas_call x1, Pallas kernels, local(): pl.pallas_call(finish, out_shape=shapes, in_specs=[hbm] * 6, out_specs=(h...  3.2 us

profile of v7, /device:TPU:55, one launch (start us, length us, event | category | flops | bytes accessed | tf_op | source)
XLA Modules:
  0.0 67.6 jit_solution(6476504038091413914)
XLA Ops:
  0.6 63.8 %move_and_update.1 = (f32[1536,128]{1,0:T(8,128)}, f32[1536,128]{1,0:T(8,128)}, f32[1536,128]{1,0:T(8,128)}, bf16[3072,128]{1,0:T(8,128)(2,1)}, bf16[2048,128]{1,0:T(8,128)(2,1)}) custom-call(s32[65]{0:T(128)} %old_off_in.1, s32[129]{0:T(256)} %off_in.1, f32[5120,128]{1,0:T(8,128)} %old_m.1, f32[5120,128]{1,0:T(8,128)} %old_f.1, f32[5120,128]{1,0:T(8,128)} %old_s.1, ...), custom_call_target="tpu_custom_call" | custom-call | tf_op jit(solution)/shard_map/move_and_update/pallas_call | solution.py:773
  64.4 3.2 %finish.1 = (f32[1536,128]{1,0:T(8,128)}, f32[1536,128]{1,0:T(8,128)}, f32[1536,128]{1,0:T(8,128)}, bf16[3072,128]{1,0:T(8,128)(2,1)}) custom-call(s32[129]{0:T(256)} %off_in.1, f32[1536,128]{1,0:T(8,128)} %get-tuple-element.13.in_m, f32[1536,128]{1,0:T(8,128)} %get-tuple-element.14.in_f, f32[1536,128]{1,0:T(8,128)} %get-tuple-element.15.in_s, ...), custom_call_target="tpu_custom_call" | custom-call | tf_op jit(solution)/shard_map/finish/pallas_call | solution.py:822

commit v8 on v7

--- a/solution.py
+++ b/solution.py
@@ -15,7 +15,7 @@
 WINDOW = 3584
 CHUNKS = 8
 SUB = 64
-EARLY = 5
+EARLY = 3
 
 
 def within(start):
@@ -353,7 +353,7 @@
         targets = targets + more * cond.astype(jnp.int32)
     pl.semaphore_wait(barrier, targets)
 
-    early = jnp.where(odd, EARLY, CHUNKS)
+    early = EARLY
 
     @pl.when(r == 1)
     def _():
@@ -464,7 +464,7 @@
                     tail_relay_in(k, rep, part).wait_recv()
                     tail_relay_out(k, rep, part).start()
 
-    @pl.when(r == 1)
+    @pl.when((r == 1) & odd)
     def _():
         @pl.loop(early, CHUNKS)
         def _(c):
@@ -478,6 +478,12 @@
         @pl.loop(0, CHUNKS)
         def _(c):
             grad_copy(c, 0).wait_recv()
+
+            @pl.when(even & (c == 0))
+            def _():
+                @pl.loop(early, CHUNKS)
+                def _(d):
+                    grad_copy(d, 1).start()
 
             @pl.when(c < passes)
             def _():
@@ -728,6 +734,9 @@
 
     for load in loads:
         load.start()
+    for load, store in zip(loads, stores):
+        load.wait()
+        store.start()
     load_off.wait()
 
     @pl.when(r == 0)
@@ -753,9 +762,6 @@
         load_low.wait()
 
     store_low.start()
-    for load, store in zip(loads, stores):
-        load.wait()
-        store.start()
     for store in stores:
         store.wait()
     store_low.wait()

time: 67.7 us -> 65.8 us (0.972)
  the two profiles are of different devices: /device:TPU:55 before, /device:TPU:8 now
where the time goes in v8:
time: 65.8 us; the launch traced here: 65.2 us
  Pallas kernels  64.6 us (98%)
    pallas_call x1, Pallas kernels, local(): pl.pallas_call(kernel, out_shape=shapes + (short,), in_specs=[hbm] * 6, o...  61.5 us
    pallas_call x1, Pallas kernels, local(): pl.pallas_call(finish, out_shape=shapes, in_specs=[hbm] * 6, out_specs=(h...  3.14 us

profile of v8, /device:TPU:8, one launch (start us, length us, event | category | flops | bytes accessed | tf_op | source)
XLA Modules:
  0.0 65.2 jit_solution(15514138842377823707)
XLA Ops:
  0.6 61.5 %move_and_update.1 = (f32[1536,128]{1,0:T(8,128)}, f32[1536,128]{1,0:T(8,128)}, f32[1536,128]{1,0:T(8,128)}, bf16[3072,128]{1,0:T(8,128)(2,1)}, bf16[2048,128]{1,0:T(8,128)(2,1)}) custom-call(s32[65]{0:T(128)} %old_off_in.1, s32[129]{0:T(256)} %off_in.1, f32[5120,128]{1,0:T(8,128)} %old_m.1, f32[5120,128]{1,0:T(8,128)} %old_f.1, f32[5120,128]{1,0:T(8,128)} %old_s.1, ...), custom_call_target="tpu_custom_call" | custom-call | tf_op jit(solution)/shard_map/move_and_update/pallas_call | solution.py:779
  62.1 3.1 %finish.1 = (f32[1536,128]{1,0:T(8,128)}, f32[1536,128]{1,0:T(8,128)}, f32[1536,128]{1,0:T(8,128)}, bf16[3072,128]{1,0:T(8,128)(2,1)}) custom-call(s32[129]{0:T(256)} %off_in.1, f32[1536,128]{1,0:T(8,128)} %get-tuple-element.13.in_m, f32[1536,128]{1,0:T(8,128)} %get-tuple-element.14.in_f, f32[1536,128]{1,0:T(8,128)} %get-tuple-element.15.in_s, ...), custom_call_target="tpu_custom_call" | custom-call | tf_op jit(solution)/shard_map/finish/pallas_call | solution.py:828

commit v9 on v8

--- a/solution.py
+++ b/solution.py
@@ -15,7 +15,8 @@
 WINDOW = 3584
 CHUNKS = 8
 SUB = 64
-EARLY = 3
+EARLY = 4
+PROMPT = 5
 
 
 def within(start):
@@ -112,11 +113,11 @@
     head_source = s - 1 + 2 * (3 - x) - turn_up
     head_rep = r
     relays_head = odd & (head_rep == 0) & (head_source >= 0)
-    tail_source = s - 1 - 2 * x + turn_down
+    tail_source = s - 2 * x + turn_down
     tail_rep = r
-    relays_tail = odd & (tail_source < count)
+    relays_tail = even & (tail_source < count) & ((x > 0) | (z_lo == 0))
     head_relays = s + jnp.where(z_lo == 0, 24, -8) + 1
-    tail_relays = s + jnp.where(z_lo == 3, -24, 8) - 6
+    tail_relays = s + jnp.where(z_lo == 3, -24, 8) - 7
 
     offsets = (
         pltpu.make_async_copy(old_off_in, old_off, off_sem.at[0]),
@@ -187,7 +188,7 @@
     def tail_relay_in(k, rep, part):
         rows = tail_place(rep)[1] // 4
         sems = (tail_sem.at[0, part, k], tail_relay_sem.at[0, k])
-        to = (r, lax.rem(s + 2 * part + 1 - turn_down + count, count))
+        to = (r, lax.rem(s + 2 * part - turn_down + count, count))
         return send(olds[k].at[pl.ds(part * rows, rows)], relay.at[1, k, pl.ds(0, rows)], sems, to)
 
     def tail_relay_out(k, rep, part):
@@ -373,9 +374,19 @@
 
         @pl.when(tail_wraps & (down_rep == rep))
         def _():
-            for part in range(4):
+            for part in (1, 2, 3):
                 for k in range(3):
                     tail_relay_in(k, rep, part).start()
+
+            @pl.when(z_lo == 0)
+            def _():
+                for k in range(3):
+                    tail_relay_in(k, rep, 0).start()
+
+            @pl.when(z_lo > 0)
+            def _():
+                for k in range(3):
+                    tail_copy(k, rep, 0).start()
 
     for copy in offsets:
         copy.wait()
@@ -399,9 +410,11 @@
         def _(j):
             pack[pl.ds(pl.multiple_of(j * SUB, SUB), SUB), :] = pack_rows(j * SUB)
 
+    prompt = jnp.where(odd & (z_lo == 3), PROMPT, CHUNKS)
+
     @pl.when(r == 0)
     def _():
-        @pl.loop(0, CHUNKS)
+        @pl.loop(0, prompt)
         def _(c):
             grad_copy(c, 0).start()
 
@@ -464,11 +477,11 @@
                     tail_relay_in(k, rep, part).wait_recv()
                     tail_relay_out(k, rep, part).start()
 
-    @pl.when((r == 1) & odd)
-    def _():
-        @pl.loop(early, CHUNKS)
-        def _(c):
-            grad_copy(c, 1).start()
+    @pl.when(r == 0)
+    def _():
+        @pl.loop(prompt, CHUNKS)
+        def _(c):
+            grad_copy(c, 0).start()
 
     passes = jnp.where(even, CHUNKS, (half - PACK) // piece)
     arrivals = jnp.where(odd, CHUNKS, (half - PACK) // piece)
@@ -479,7 +492,7 @@
         def _(c):
             grad_copy(c, 0).wait_recv()
 
-            @pl.when(even & (c == 0))
+            @pl.when(c == 0)
             def _():
                 @pl.loop(early, CHUNKS)
                 def _(d):

time: 65.8 us -> 65.4 us (level)
  the two profiles are of different devices: /device:TPU:8 before, /device:TPU:57 now
where the time goes in v9:
time: 65.4 us; the launch traced here: 65.3 us
  Pallas kernels  64.7 us (99%)
    pallas_call x1, Pallas kernels, local(): pl.pallas_call(kernel, out_shape=shapes + (short,), in_specs=[hbm] * 6, o...  61.6 us
    pallas_call x1, Pallas kernels, local(): pl.pallas_call(finish, out_shape=shapes, in_specs=[hbm] * 6, out_specs=(h...  3.14 us

profile of v9, /device:TPU:57, one launch (start us, length us, event | category | flops | bytes accessed | tf_op | source)
XLA Modules:
  0.0 65.3 jit_solution(8919446803371159005)
XLA Ops:
  0.6 61.6 %move_and_update.1 = (f32[1536,128]{1,0:T(8,128)}, f32[1536,128]{1,0:T(8,128)}, f32[1536,128]{1,0:T(8,128)}, bf16[3072,128]{1,0:T(8,128)(2,1)}, bf16[2048,128]{1,0:T(8,128)(2,1)}) custom-call(s32[65]{0:T(128)} %old_off_in.1, s32[129]{0:T(256)} %off_in.1, f32[5120,128]{1,0:T(8,128)} %old_m.1, f32[5120,128]{1,0:T(8,128)} %old_f.1, f32[5120,128]{1,0:T(8,128)} %old_s.1, ...), custom_call_target="tpu_custom_call" | custom-call | tf_op jit(solution)/shard_map/move_and_update/pallas_call | solution.py:792
  62.2 3.1 %finish.1 = (f32[1536,128]{1,0:T(8,128)}, f32[1536,128]{1,0:T(8,128)}, f32[1536,128]{1,0:T(8,128)}, bf16[3072,128]{1,0:T(8,128)(2,1)}) custom-call(s32[129]{0:T(256)} %off_in.1, f32[1536,128]{1,0:T(8,128)} %get-tuple-element.13.in_m, f32[1536,128]{1,0:T(8,128)} %get-tuple-element.14.in_f, f32[1536,128]{1,0:T(8,128)} %get-tuple-element.15.in_s, ...), custom_call_target="tpu_custom_call" | custom-call | tf_op jit(solution)/shard_map/finish/pallas_call | solution.py:841

commit v10 on v9

--- a/solution.py
+++ b/solution.py
@@ -119,6 +119,9 @@
     head_relays = s + jnp.where(z_lo == 0, 24, -8) + 1
     tail_relays = s + jnp.where(z_lo == 3, -24, 8) - 7
 
+    barrier = pltpu.get_barrier_semaphore()
+    pl.semaphore_signal(barrier, inc=1, device_id=other, device_id_type=MESH)
+
     offsets = (
         pltpu.make_async_copy(old_off_in, old_off, off_sem.at[0]),
         pltpu.make_async_copy(new_off_in, new_off, off_sem.at[1]),
@@ -309,8 +312,6 @@
     def _():
         far_copy(1, grad_rows).start()
 
-    barrier = pltpu.get_barrier_semaphore()
-    pl.semaphore_signal(barrier, inc=1, device_id=other, device_id_type=MESH)
 
     pl.semaphore_signal(barrier, inc=1, device_id=die_to, device_id_type=MESH)
 

time: 65.4 us -> 65.4 us (level)
  no operation moved by 1% of the time
where the time goes in v10:
time: 65.4 us; the launch traced here: 65.3 us
  Pallas kernels  64.6 us (99%)
    pallas_call x1, Pallas kernels, local(): pl.pallas_call(kernel, out_shape=shapes + (short,), in_specs=[hbm] * 6, o...  61.5 us
    pallas_call x1, Pallas kernels, local(): pl.pallas_call(finish, out_shape=shapes, in_specs=[hbm] * 6, out_specs=(h...  3.14 us

profile of v10, /device:TPU:57, one launch (start us, length us, event | category | flops | bytes accessed | tf_op | source)
XLA Modules:
  0.0 65.3 jit_solution(10149468035489016750)
XLA Ops:
  0.6 61.5 %move_and_update.1 = (f32[1536,128]{1,0:T(8,128)}, f32[1536,128]{1,0:T(8,128)}, f32[1536,128]{1,0:T(8,128)}, bf16[3072,128]{1,0:T(8,128)(2,1)}, bf16[2048,128]{1,0:T(8,128)(2,1)}) custom-call(s32[65]{0:T(128)} %old_off_in.1, s32[129]{0:T(256)} %off_in.1, f32[5120,128]{1,0:T(8,128)} %old_m.1, f32[5120,128]{1,0:T(8,128)} %old_f.1, f32[5120,128]{1,0:T(8,128)} %old_s.1, ...), custom_call_target="tpu_custom_call" | custom-call | tf_op jit(solution)/shard_map/move_and_update/pallas_call | solution.py:793
  62.1 3.1 %finish.1 = (f32[1536,128]{1,0:T(8,128)}, f32[1536,128]{1,0:T(8,128)}, f32[1536,128]{1,0:T(8,128)}, bf16[3072,128]{1,0:T(8,128)(2,1)}) custom-call(s32[129]{0:T(256)} %off_in.1, f32[1536,128]{1,0:T(8,128)} %get-tuple-element.13.in_m, f32[1536,128]{1,0:T(8,128)} %get-tuple-element.14.in_f, f32[1536,128]{1,0:T(8,128)} %get-tuple-element.15.in_s, ...), custom_call_target="tpu_custom_call" | custom-call | tf_op jit(solution)/shard_map/finish/pallas_call | solution.py:842

commit v11 on v9

--- a/solution.py
+++ b/solution.py
@@ -15,7 +15,7 @@
 WINDOW = 3584
 CHUNKS = 8
 SUB = 64
-EARLY = 4
+EARLY = 5
 PROMPT = 5
 
 
@@ -492,7 +492,7 @@
         def _(c):
             grad_copy(c, 0).wait_recv()
 
-            @pl.when(c == 0)
+            @pl.when(c == 1)
             def _():
                 @pl.loop(early, CHUNKS)
                 def _(d):

time: 65.4 us -> 65.4 us (level)
  the two profiles are of different devices: /device:TPU:57 before, /device:TPU:7 now
where the time goes in v11:
time: 65.4 us; the launch traced here: 65.3 us
  Pallas kernels  64.7 us (99%)
    pallas_call x1, Pallas kernels, local(): pl.pallas_call(kernel, out_shape=shapes + (short,), in_specs=[hbm] * 6, o...  61.5 us
    pallas_call x1, Pallas kernels, local(): pl.pallas_call(finish, out_shape=shapes, in_specs=[hbm] * 6, out_specs=(h...  3.14 us

profile of v11, /device:TPU:7, one launch (start us, length us, event | category | flops | bytes accessed | tf_op | source)
XLA Modules:
  0.0 65.3 jit_solution(3176871600197285643)
XLA Ops:
  0.6 61.5 %move_and_update.1 = (f32[1536,128]{1,0:T(8,128)}, f32[1536,128]{1,0:T(8,128)}, f32[1536,128]{1,0:T(8,128)}, bf16[3072,128]{1,0:T(8,128)(2,1)}, bf16[2048,128]{1,0:T(8,128)(2,1)}) custom-call(s32[65]{0:T(128)} %old_off_in.1, s32[129]{0:T(256)} %off_in.1, f32[5120,128]{1,0:T(8,128)} %old_m.1, f32[5120,128]{1,0:T(8,128)} %old_f.1, f32[5120,128]{1,0:T(8,128)} %old_s.1, ...), custom_call_target="tpu_custom_call" | custom-call | tf_op jit(solution)/shard_map/move_and_update/pallas_call | solution.py:792
  62.2 3.1 %finish.1 = (f32[1536,128]{1,0:T(8,128)}, f32[1536,128]{1,0:T(8,128)}, f32[1536,128]{1,0:T(8,128)}, bf16[3072,128]{1,0:T(8,128)(2,1)}) custom-call(s32[129]{0:T(256)} %off_in.1, f32[1536,128]{1,0:T(8,128)} %get-tuple-element.13.in_m, f32[1536,128]{1,0:T(8,128)} %get-tuple-element.14.in_f, f32[1536,128]{1,0:T(8,128)} %get-tuple-element.15.in_s, ...), custom_call_target="tpu_custom_call" | custom-call | tf_op jit(solution)/shard_map/finish/pallas_call | solution.py:841
